TPU v7x, 1024 devices: a whole 8x8x8 slice. The times are simulated.
1024 devices in a mesh: gx: 64 (over z, y), gy: 16 (over x, core).
Axes of the slice: x: 8, y: 8, z: 8, core: 2. Of those that a mesh axis runs over, the one named last changes fastest.
Arguments:
- coarse_state: float32 [5, 2, 4096, 2048], P(None, None, 'gx', 'gy'), as said below
- fine_state: float32 [64, 16, 8, 5, 4, 256], P('gx', 'gy'), as said below
- source_rows: int32 [64, 16, 8], P(None, 'gy'), may hold values from 0 to 63, as said below
- tile_ids: int32 [64, 16, 8], P(None, 'gy'), may hold values from 17 to 110, as said below
Outputs:
- coarse_out: float32 [5, 2, 4096, 2048], P(None, None, 'gx', 'gy')
- fine_out: float32 [64, 16, 8, 5, 4, 256], P('gx', 'gy')
Inputs may be any that keep to these rules, and one draw needn't show every extreme that they name: `coarse_state`: fields are density, the three momenta and energy of a gas of adiabatic index 1.4; density and pressure lie between 0.5 and 2 and each velocity component between -0.5 and 0.5. `fine_state`: as for coarse_state. `source_rows`: entry [o, j, r] is the gx index of the device in grid column j whose block the fine box r of device (o, j) refines. Among the 8 entries of one device no value appears more than 1 times, and some value appears exactly 1 times. `tile_ids`: tile t covers the 8 x 8 coarse cells from row (t // 16) * 8 and column (t % 16) * 8 of the source device's block. No tile lies in the outermost cycle of tiles of a block (1 <= t // 16 <= 6 and 1 <= t % 16 <= 14), and no pair of source and tile occurs twice in one grid column.
All inputs are finite; a program needn't handle non-finite values.
Results may differ from a plain program's by a relative error of at most 0.0003.
Values sent between devices are 32-bit elements; how exact they have to be, the bound alone decides.
A program may use at most 64 MiB of HBM per device.

v0:
```python
import functools

import jax
import jax.numpy as jnp
from jax import lax
from jax.experimental import pallas as pl
from jax.experimental.pallas import tpu as pltpu
from jax.sharding import PartitionSpec as P

MESH = pl.DeviceIdType.MESH
HEAT_RATIO = 1.4
HALF_STEP = 0.025
BOXES = 8
IMAGES = 10
ROWS = 64
LANES = 128


def iota(shape, dim):
    return lax.broadcasted_iota(jnp.int32, shape, dim)


def roll(x, shift, axis):
    if isinstance(shift, int):
        shift = shift % x.shape[axis]
        if shift == 0:
            return x
    return pltpu.roll(x, shift, axis)


def primitives(u):
    inverse = 1.0 / u[0]
    velocity = [u[1] * inverse, u[2] * inverse, u[3] * inverse]
    kinetic = 0.5 * (u[1] * velocity[0] + u[2] * velocity[1] + u[3] * velocity[2])
    pressure = (HEAT_RATIO - 1.0) * (u[4] - kinetic)
    sound = jnp.sqrt(HEAT_RATIO * pressure * inverse)
    return velocity, pressure, sound


def scaled_state(u, velocity, pressure, sound, k):
    drift = HALF_STEP * velocity[k]
    speed = HALF_STEP * (jnp.abs(velocity[k]) + sound)
    return list(u) + [pressure, drift, speed]


def scaled_flux(state, k):
    u, pressure, drift = state[:5], state[5], state[6]
    flux = [u[f] * drift for f in range(5)]
    flux[1 + k] = flux[1 + k] + HALF_STEP * pressure
    flux[4] = (u[4] + pressure) * drift
    return flux


def face_flux(left, right, k):
    a, b = scaled_flux(left, k), scaled_flux(right, k)
    top = jnp.maximum(left[7], right[7])
    return [(a[f] + b[f]) - top * (right[f] - left[f]) for f in range(5)]


def coarse_step(img, flux_x, flux_y):
    first_row = iota((ROWS, LANES), 0) == 0
    first_col = iota((ROWS, LANES), 1) == 0
    cells, prims = [], []
    for z in range(2):
        u = [img[pl.ds((2 * f + z) * ROWS, ROWS), :] for f in range(5)]
        cells.append(u)
        prims.append(primitives(u))
    depth = [HALF_STEP * (jnp.abs(prims[z][0][0]) + prims[z][2]) for z in range(2)]
    depth = 2.0 * jnp.maximum(depth[0], depth[1])
    for z in range(2):
        u = cells[z]
        new = [u[f] - depth * (u[f] - cells[1 - z][f]) for f in range(5)]
        for k, axis, first, saved in ((1, 0, first_row, flux_x), (2, 1, first_col, flux_y)):
            state = scaled_state(u, *prims[z], k)
            before = [roll(s, 1, axis) for s in state]
            faces = face_flux(before, state, k)
            for f in range(5):
                face = jnp.where(first, 0.0, faces[f])
                saved[pl.ds((2 * f + z) * ROWS, ROWS), :] = face
                new[f] = new[f] - (roll(face, -1, axis) - face)
        for f in range(5):
            img[pl.ds((IMAGES + 2 * f + z) * ROWS, ROWS), :] = new[f]


def build_tables(img, turned, table_x, table_y):
    for tx in range(1, 7):
        for k, row in ((0, 8 * tx - 1), (1, 8 * tx + 8)):
            table_x[tx, pl.ds(16 * k, 8), :] = img[pl.ds(row, 8, stride=ROWS), :]
            table_x[tx, pl.ds(16 * k + 8, 8), :] = img[pl.ds(8 * ROWS + row, 8, stride=ROWS), :]
            table_x[tx, pl.ds(32 + 4 * k, 4), :] = img[pl.ds(16 * ROWS + row, 4, stride=ROWS), :]
    for p in range(IMAGES):
        turned[pl.ds(p * LANES, LANES), :] = jnp.transpose(img[pl.ds(p * LANES, LANES), :])
    for ty in range(1, 15):
        for k, col in ((0, 8 * ty - 1), (1, 8 * ty + 8)):
            table_y[ty, pl.ds(8 * k, 8), :] = turned[pl.ds(col, 8, stride=LANES), :]
            table_y[ty, pl.ds(16 + 2 * k, 2), :] = turned[pl.ds(8 * LANES + col, 2, stride=LANES), :]


def wanted_tile(sources, tiles, o, me):
    tile = jnp.int32(0)
    for r in range(BOXES):
        tile = jnp.where(sources[o, r] == me, tiles[o, r], tile)
    return tile


def pack_rims(n, me, sources, tiles, table_x, table_y, by_tile, rims):
    group = iota((8, LANES), 1) // 8
    for tx in range(1, 7):
        for ty in range(1, 15):
            message = jnp.zeros((8, LANES), jnp.float32)
            for g in range(5):
                part = roll(table_x[tx, pl.ds(8 * g, 8), :], 8 * g - 8 * ty, 1)
                message = jnp.where(group == g, part, message)
            for u in range(3):
                columns = table_y[ty, pl.ds(8 * u, 8), :]
                for j in range(2):
                    part = roll(columns, 64 + 16 * u + 8 * j - 64 * j - 8 * tx, 1)
                    message = jnp.where(group == 8 + 2 * u + j, part, message)
            by_tile[16 * tx + ty] = message

    def one(o, carry):
        rims[o] = by_tile[jnp.maximum(wanted_tile(sources, tiles, o, me), 17)]
        return carry

    lax.fori_loop(0, n, one, 0)


def pack_halo(img, halo_rows, halo_cols):
    halo_rows[...] = jnp.zeros_like(halo_rows)
    halo_rows[pl.ds(0, 8), :] = img[pl.ds(0, 8, stride=ROWS), :]
    halo_rows[pl.ds(8, 2), :] = img[pl.ds(8 * ROWS, 2, stride=ROWS), :]
    halo_rows[pl.ds(16, 8), :] = img[pl.ds(ROWS - 1, 8, stride=ROWS), :]
    halo_rows[pl.ds(24, 2), :] = img[pl.ds(9 * ROWS - 1, 2, stride=ROWS), :]
    lane = iota((ROWS, LANES), 1)
    packed = jnp.ones((ROWS, LANES), jnp.float32)
    for image in range(IMAGES):
        cells = img[pl.ds(image * ROWS, ROWS), :]
        packed = jnp.where(lane == image, roll(cells, image, 1), packed)
        packed = jnp.where(lane == 16 + image, roll(cells, 17 + image, 1), packed)
    halo_cols[...] = packed


def finish_edges(img, halo_rows, halo_cols, from_rows, from_cols):
    def by_row(source, start):
        u = [source[pl.ds(start + 2 * f, 2), :] for f in range(5)]
        return scaled_state(u, *primitives(u), 1)

    own_low, own_high = by_row(halo_rows, 0), by_row(halo_rows, 16)
    low = face_flux(by_row(from_rows.at[0], 16), own_low, 1)
    high = face_flux(own_high, by_row(from_rows.at[1], 0), 1)
    for f in range(5):
        for z in range(2):
            base = (IMAGES + 2 * f + z) * ROWS
            first, last = pl.ds(base, 1), pl.ds(base + ROWS - 1, 1)
            img[first, :] = img[first, :] + low[f][z : z + 1]
            img[last, :] = img[last, :] - high[f][z : z + 1]

    lane = iota((ROWS, LANES), 1)
    own = halo_cols[...]
    left = jnp.where(lane < 16, roll(from_cols[0], -16, 1), own)
    right = jnp.where(lane < 16, own, roll(from_cols[1], 16, 1))

    def by_lane(packed):
        u = [roll(packed, -2 * f, 1) for f in range(5)]
        return scaled_state(u, *primitives(u), 2)

    faces = face_flux(by_lane(left), by_lane(right), 2)
    for f in range(5):
        for z in range(2):
            rows = pl.ds((IMAGES + 2 * f + z) * ROWS, ROWS)
            cells = img[rows, :]
            cells = jnp.where(lane == 0, cells + roll(faces[f], -z, 1), cells)
            cells = jnp.where(lane == LANES - 1, cells - roll(faces[f], 111 - z, 1), cells)
            img[rows, :] = cells


def own_rims(me, sources, rims, held):
    for r in range(BOXES):
        held[pl.ds(8 * r, 8), :] = rims[sources[me, r]]
    by_row = [held[pl.ds(s, BOXES, stride=8), :] for s in range(8)]
    lane = iota((BOXES, LANES), 1)

    def pair(low, low_lane, high, high_lane):
        first = roll(low, -low_lane, 1)
        second = roll(high, 8 - high_lane, 1)
        return jnp.where(lane < 8, first, jnp.where(lane < 16, second, 0.0))

    sides = [[], []]
    for image in range(2 * IMAGES):
        s, g = image % 8, image // 8
        if g < 2:
            sides[0].append(pair(by_row[s], 8 * g, by_row[s], 8 * (g + 2)))
        else:
            sides[0].append(pair(by_row[s], 32, by_row[s + 4], 32))
        p, j = image // 2, image % 2
        if p < 8:
            sides[1].append(pair(by_row[p], 64 + 8 * j, by_row[p], 80 + 8 * j))
        else:
            sides[1].append(pair(by_row[p - 8], 96 + 8 * j, by_row[p - 6], 96 + 8 * j))

    source, cell = iota((LANES, 256), 0), iota((LANES, 256), 1)
    a, b = cell // 16, cell % 16
    spread = []
    for side, (along, across) in enumerate(((b, a), (a, b))):
        chosen = (source < 16) & (source % 8 == along // 2) & (source // 8 == across // 8)
        weights = jnp.where(chosen, 1.0, 0.0)
        old = sides[side][:IMAGES]
        mid = [0.5 * (x + y) for x, y in zip(old, sides[side][IMAGES:])]
        ghosts = jnp.dot(
            jnp.concatenate(old + mid, axis=0),
            weights,
            precision=lax.Precision.HIGHEST,
            preferred_element_type=jnp.float32,
        )
        spread.append(
            [
                [ghosts[(IMAGES * t + i) * 8 : (IMAGES * t + i) * 8 + 8] for i in range(IMAGES)]
                for t in range(2)
            ]
        )
    return spread


def fine_step(u, ghosts_x, ghosts_y, edges):
    cell = iota((BOXES, 256), 1)
    a, b = cell // 16, cell % 16
    prims = [primitives([u[f][z] for f in range(5)]) for z in range(4)]
    states = [scaled_state([u[f][z] for f in range(5)], *prims[z], 0) for z in range(4)]
    deep = [face_flux(states[z], states[(z + 1) % 4], 0) for z in range(4)]
    new = [[u[f][z] - (deep[z][f] - deep[z - 1][f]) for z in range(4)] for f in range(5)]
    sides = (
        (1, ghosts_x, 16, a == 0, a == 15, a < 8),
        (2, ghosts_y, 1, b == 0, b == 15, b < 8),
    )
    for side, (k, ghosts, stride, first, last, lower) in enumerate(sides):
        for half in range(2):
            cells = [ghosts[2 * f + half] for f in range(5)]
            ghost = scaled_state(cells, *primitives(cells), k)
            for z in (2 * half, 2 * half + 1):
                state = scaled_state([u[f][z] for f in range(5)], *prims[z], k)
                before = [
                    jnp.where(first, ghost[i], roll(state[i], stride, 1)) for i in range(8)
                ]
                low = face_flux(before, state, k)
                outer = face_flux(state, ghost, k)
                for f in range(5):
                    high = jnp.where(last, outer[f], roll(low[f], -stride, 1))
                    new[f][z] = new[f][z] - (high - low[f])
                    edge = jnp.where(lower, low[f], high)
                    held = edges[side][2 * f + half]
                    edges[side][2 * f + half] = edge if held is None else held + edge
    return new


def pack_results(n, me, sources, u, edges, held, packed, results):
    cell, target = iota((256, LANES), 0), iota((256, LANES), 1)
    a, b = cell // 16, cell % 16
    flipped, along = 7 - a // 2, b // 2
    average = (target < 64) & (target // 8 == flipped) & (target % 8 == along)
    rows = ((target // 8 == 8) & (a == 0) | (target // 8 == 9) & (a == 15)) & (target % 8 == along)
    cols = ((target // 8 == 10) & (b == 0) | (target // 8 == 11) & (b == 15)) & (
        target % 8 == flipped
    )
    thick = [u[i // 2][2 * (i % 2)] + u[i // 2][2 * (i % 2) + 1] for i in range(IMAGES)]
    total = None
    for values, weights in ((thick, average), (edges[0], rows), (edges[1], cols)):
        part = jnp.dot(
            jnp.concatenate(values, axis=0),
            jnp.where(weights, 0.125, 0.0),
            precision=lax.Precision.HIGHEST,
            preferred_element_type=jnp.float32,
        )
        total = part if total is None else total + part
    sums = [total[8 * i : 8 * i + 8] for i in range(IMAGES)]
    lane = iota((BOXES, LANES), 1)
    for q in range(5):
        row = jnp.where(lane < 64, sums[2 * q], roll(sums[2 * q + 1], 64, 1))
        held[pl.ds(q, BOXES, stride=8), :] = row
    for w in range(3):
        row = jnp.zeros((BOXES, LANES), jnp.float32)
        for h in range(4):
            if 4 * w + h < IMAGES:
                row = jnp.where(lane // 32 == h, roll(sums[4 * w + h], 32 * h - 64, 1), row)
        held[pl.ds(5 + w, BOXES, stride=8), :] = row

    for r in range(BOXES):
        packed[r] = held[pl.ds(8 * r, 8), :]

    def one(s, carry):
        box = jnp.int32(0)
        for r in range(BOXES):
            box = jnp.where(sources[me, r] == s, r, box)
        results[s] = packed[box]
        return carry

    lax.fori_loop(0, n, one, 0)


def exchange(n, me, source, target, sems):
    def send(step, carry):
        other = lax.rem(me + step, n)
        pltpu.make_async_remote_copy(
            src_ref=source.at[other],
            dst_ref=target.at[me],
            send_sem=sems.at[0],
            recv_sem=sems.at[1],
            device_id={"gx": other},
            device_id_type=MESH,
        ).start()
        return carry

    lax.fori_loop(1, n, send, 0)
    return pltpu.make_async_remote_copy(
        src_ref=source.at[pl.ds(0, n - 1)],
        dst_ref=target.at[pl.ds(0, n - 1)],
        send_sem=sems.at[0],
        recv_sem=sems.at[1],
        device_id={"gx": me},
        device_id_type=MESH,
    )


def level_kernel(
    n,
    m,
    coarse,
    fine,
    sources,
    tiles,
    coarse_new,
    rows_x,
    flux_y,
    returned,
    fine_out,
    img,
    flux_x,
    turned,
    table_x,
    table_y,
    by_tile,
    rims,
    rims_in,
    held,
    packed,
    results,
    cells,
    halo_rows,
    halo_cols,
    from_rows,
    from_cols,
    rim_sems,
    result_sems,
    halo_sems,
):
    me, column = lax.axis_index("gx"), lax.axis_index("gy")
    up, down = lax.rem(me + 1, n), lax.rem(me + n - 1, n)
    right, left = lax.rem(column + 1, m), lax.rem(column + m - 1, m)
    barrier = pltpu.get_barrier_semaphore()

    def greet(step, carry):
        other = lax.rem(me + step, n)
        pl.semaphore_signal(barrier, 1, device_id={"gx": other}, device_id_type=MESH)
        return carry

    lax.fori_loop(1, n, greet, 0)
    pl.semaphore_signal(barrier, 1, device_id={"gy": right}, device_id_type=MESH)
    pl.semaphore_signal(barrier, 1, device_id={"gy": left}, device_id_type=MESH)

    img[pl.ds(0, IMAGES * ROWS), :] = coarse[...]
    coarse_step(img, flux_x, flux_y)
    table_x[...] = jnp.zeros_like(table_x)
    table_y[...] = jnp.zeros_like(table_y)
    build_tables(img, turned, table_x, table_y)
    pack_rims(n, me, sources, tiles, table_x, table_y, by_tile, rims)
    pack_halo(img, halo_rows, halo_cols)
    pl.semaphore_wait(barrier, n + 1)

    rim_copies = exchange(n, me, rims, rims_in, rim_sems)
    halos = []
    for i, (source, target, where) in enumerate(
        (
            (halo_rows, from_rows.at[0], {"gx": up}),
            (halo_rows, from_rows.at[1], {"gx": down}),
            (halo_cols, from_cols.at[0], {"gy": right}),
            (halo_cols, from_cols.at[1], {"gy": left}),
        )
    ):
        copy = pltpu.make_async_remote_copy(
            src_ref=source,
            dst_ref=target,
            send_sem=halo_sems.at[0, i],
            recv_sem=halo_sems.at[1, i],
            device_id=where,
            device_id_type=MESH,
        )
        copy.start()
        halos.append(copy)
    for r in range(BOXES):
        for f in range(5):
            for z in range(4):
                cells[4 * f + z, pl.ds(r, 1), :] = fine[r, f, pl.ds(z, 1), :]
    for i in range(8):
        for image in range(IMAGES):
            rows_x[i, pl.ds(image, 1), :] = flux_x[pl.ds(image * ROWS + 8 * i, 1), :]
    rows_x[:, pl.ds(IMAGES, 6), :] = jnp.zeros((8, 6, LANES), jnp.float32)
    for copy in halos:
        copy.wait_recv()
    finish_edges(img, halo_rows, halo_cols, from_rows, from_cols)
    coarse_new[...] = img[pl.ds(IMAGES * ROWS, IMAGES * ROWS), :]

    rim_copies.wait_recv()
    rims_in[me] = rims[me]
    ghosts = own_rims(me, sources, rims_in, held)
    u = [[cells[4 * f + z] for z in range(4)] for f in range(5)]
    edges = [[None] * IMAGES, [None] * IMAGES]
    u = fine_step(u, ghosts[0][0], ghosts[1][0], edges)
    u = fine_step(u, ghosts[0][1], ghosts[1][1], edges)
    pack_results(n, me, sources, u, edges, held, packed, results)
    result_copies = exchange(n, me, results, returned, result_sems)
    for f in range(5):
        for z in range(4):
            for r in range(BOXES):
                fine_out[r, f, pl.ds(z, 1), :] = u[f][z][r : r + 1]
    rim_copies.wait_send()
    for copy in halos:
        copy.wait_send()
    result_copies.wait_recv()
    returned[me] = results[me]
    result_copies.wait_send()


def merge_kernel(n, new, rows_x, flux_y, returned, sources, tiles, fine, out, fine_out):
    me = lax.axis_index("gx")
    out[...] = new[...]
    fine_out[...] = fine[...]
    lane, sub = iota((8, LANES), 1), iota((8, LANES), 0)

    def spread(o, row):
        return jnp.broadcast_to(returned[o, pl.ds(row, 1), :], (8, LANES))

    def turned(x, shift, stride):
        x = pltpu.roll(x, 0, 1, stride=stride, stride_axis=0)
        return pltpu.roll(x, lax.rem(shift + 2 * LANES, LANES), 1)

    def correct(o, carry):
        tile = wanted_tile(sources, tiles, o, me)

        @pl.when(tile > 0)
        def _():
            tx, ty = tile // 16, tile % 16
            inside = lane // 8 == ty
            low_face = rows_x[tx]
            high_face = rows_x[tx + 1]
            for image in range(IMAGES):
                base = 32 * (image % 4)
                values = spread(o, 5 + image // 4)
                here = image * ROWS + 8 * tx
                rows = pl.ds(pl.multiple_of(here - 8, 8), 8)
                low = pltpu.roll(values, lax.rem(8 * ty - base + LANES, LANES), 1)
                change = low - low_face[image : image + 1]
                out[rows, :] = out[rows, :] - jnp.where(inside & (sub == 7), change, 0.0)
                rows = pl.ds(pl.multiple_of(here + 8, 8), 8)
                high = pltpu.roll(values, lax.rem(8 * ty - base - 8 + 2 * LANES, LANES), 1)
                change = high - high_face[image : image + 1]
                out[rows, :] = out[rows, :] + jnp.where(inside & (sub == 0), change, 0.0)
                rows = pl.ds(pl.multiple_of(here, 8), 8)
                faces = flux_y[rows, :]
                low = turned(values, 8 * ty - 1 - base - 23, 1) - pltpu.roll(faces, LANES - 1, 1)
                high = turned(values, 8 * ty + 8 - base - 31, 1) - faces
                change = jnp.where(lane == 8 * ty + 8, high, 0.0)
                change = jnp.where(lane == 8 * ty - 1, -low, change)
                out[rows, :] = out[rows, :] + change

        return carry

    def average(o, carry):
        tile = wanted_tile(sources, tiles, o, me)

        @pl.when(tile > 0)
        def _():
            tx, ty = tile // 16, tile % 16
            inside = lane // 8 == ty
            for image in range(IMAGES):
                rows = pl.ds(pl.multiple_of(image * ROWS + 8 * tx, 8), 8)
                values = turned(spread(o, image // 2), 8 * ty - 64 * (image % 2) - 56, 8)
                out[rows, :] = jnp.where(inside, values, out[rows, :])

        return carry

    lax.fori_loop(0, n, correct, 0)
    lax.fori_loop(0, n, average, 0)


def body(n, m, coarse_state, fine_state, source_rows, tile_ids):
    vmem = pl.BlockSpec(memory_space=pltpu.VMEM)
    smem = pl.BlockSpec(memory_space=pltpu.SMEM)
    f32 = jnp.float32
    coarse = coarse_state.reshape(IMAGES * ROWS, LANES)
    fine = fine_state.reshape(BOXES, 5, 4, 256)
    sources = source_rows.reshape(n, BOXES)
    tiles = tile_ids.reshape(n, BOXES)
    shape = jax.ShapeDtypeStruct
    new, rows_x, flux_y, returned, fine_out = pl.pallas_call(
        functools.partial(level_kernel, n, m),
        out_shape=(
            shape((IMAGES * ROWS, LANES), f32),
            shape((8, 16, LANES), f32),
            shape((IMAGES * ROWS, LANES), f32),
            shape((n, 8, LANES), f32),
            shape((BOXES, 5, 4, 256), f32),
        ),
        in_specs=[vmem, vmem, smem, smem],
        out_specs=(vmem,) * 5,
        scratch_shapes=[
            pltpu.VMEM((2 * IMAGES * ROWS, LANES), f32),
            pltpu.VMEM((IMAGES * ROWS, LANES), f32),
            pltpu.VMEM((IMAGES * LANES, LANES), f32),
            pltpu.VMEM((8, 40, LANES), f32),
            pltpu.VMEM((16, 24, LANES), f32),
            pltpu.VMEM((128, 8, LANES), f32),
            pltpu.VMEM((n, 8, LANES), f32),
            pltpu.VMEM((n, 8, LANES), f32),
            pltpu.VMEM((8 * BOXES, LANES), f32),
            pltpu.VMEM((BOXES, 8, LANES), f32),
            pltpu.VMEM((n, 8, LANES), f32),
            pltpu.VMEM((20, BOXES, 256), f32),
            pltpu.VMEM((32, LANES), f32),
            pltpu.VMEM((ROWS, LANES), f32),
            pltpu.VMEM((2, 32, LANES), f32),
            pltpu.VMEM((2, ROWS, LANES), f32),
            pltpu.SemaphoreType.DMA((2,)),
            pltpu.SemaphoreType.DMA((2,)),
            pltpu.SemaphoreType.DMA((2, 4)),
        ],
        compiler_params=pltpu.CompilerParams(
            collective_id=0, has_side_effects=True, vmem_limit_bytes=40 * 1024 * 1024
        ),
        name="levels",
    )(coarse, fine, sources, tiles)
    out, fine_out = pl.pallas_call(
        functools.partial(merge_kernel, n),
        out_shape=(
            shape((IMAGES * ROWS, LANES), f32),
            shape((BOXES, 5, 4, 256), f32),
        ),
        in_specs=[vmem, vmem, vmem, vmem, smem, smem, vmem],
        out_specs=(vmem,) * 2,
        compiler_params=pltpu.CompilerParams(vmem_limit_bytes=40 * 1024 * 1024),
        name="merge",
    )(new, rows_x, flux_y, returned, sources, tiles, fine_out)
    return out.reshape(coarse_state.shape), fine_out.reshape(fine_state.shape)


def solution(mesh):
    return jax.shard_map(
        functools.partial(body, mesh.shape["gx"], mesh.shape["gy"]),
        mesh=mesh,
        in_specs=(
            P(None, None, "gx", "gy"),
            P("gx", "gy", None, None, None, None),
            P(None, "gy", None),
            P(None, "gy", None),
        ),
        out_specs=(P(None, None, "gx", "gy"), P("gx", "gy", None, None, None, None)),
        check_vma=False,
    )
```

profile of v0, /device:TPU:2, one launch (start us, length us, event | category | flops | bytes accessed | tf_op | source)
XLA Modules:
  0.0 62.6 jit_solution(15170502186299460243)
XLA Ops:
  0.6 0.0 copy-start.2
  0.6 0.8 %copy.6 = s32[64,1,8]{2,0,1:T(8,128)S(1)} copy(s32[64,1,8]{0,2,1:T(8,128)} %param.6) | data formatting | bytes 4096 | tf_op args[2]
  1.4 0.0 copy-done.2
  1.4 0.1 copy.7
  1.5 0.0 copy-start
  1.5 1.0 %copy-done = f32[5,2,64,128]{3,2,1,0:T(8,128)S(1)} copy-done((f32[5,2,64,128]{3,2,1,0:T(8,128)S(1)}, f32[5,2,64,128]{3,2,1,0:T(8,128)}, u32[]{:S(2)}) %copy-start) | copy-done | bytes 327704
  2.5 0.0 copy-start.1
  2.5 0.9 %copy-done.1 = f32[1,1,8,5,4,256]{5,4,3,2,1,0:T(4,128)S(1)} copy-done((f32[1,1,8,5,4,256]{5,4,3,2,1,0:T(4,128)S(1)}, f32[1,1,8,5,4,256]{5,4,3,2,1,0:T(4,128)}, u32[]{:S(2)}) %copy-start.1) | copy-done | bytes 163864
  3.4 44.8 %levels.1 = (f32[640,128]{1,0:T(8,128)S(1)}, f32[8,16,128]{2,1,0:T(8,128)S(1)}, f32[640,128]{1,0:T(8,128)S(1)}, f32[64,8,128]{2,1,0:T(8,128)S(1)}, f32[8,5,4,256]{3,2,1,0:T(4,128)S(1)}) custom-call(f32[640,128]{1,0:T(8,128)S(1)} %bitcast.6, f32[8,5,4,256]{3,2,1,0:T(4,128)S(1)} %bitcast.11, s32[64,8]{1,0:T(8,128)S(1)} %bitcast.7, s32[64,8]{1,0:T(8,128)S(1)} %bitcast.9), custom_call_target="tpu_custom_call" | custom-call | tf_op jit(solution)/shard_map/levels/pallas_call | solution.py:503
  48.3 14.3 %merge.1 = (f32[640,128]{1,0:T(8,128)}, f32[8,5,4,256]{3,2,1,0:T(4,128)}) custom-call(f32[640,128]{1,0:T(8,128)S(1)} %get-tuple-element.9.new, f32[8,16,128]{2,1,0:T(8,128)S(1)} %get-tuple-element.10.rows_x, f32[640,128]{1,0:T(8,128)S(1)} %get-tuple-element.11.flux_y, f32[64,8,128]{2,1,0:T(8,128)S(1)} %get-tuple-element.12.returned, s32[64,8]{1,0:T(8,128)S(1)} %bitcast.8, ...), custom_call_target="tpu_custom_call" | custom-call | tf_op jit(solution)/shard_map/merge/pallas_call | solution.py:540
Async XLA Ops:
  0.6 0.8 %copy-start.2 = (s32[64,1,8]{0,2,1:T(8,128)S(1)}, s32[64,1,8]{0,2,1:T(8,128)}, u32[]{:S(2)}) copy-start(s32[64,1,8]{0,2,1:T(8,128)} %param.7) | copy-start | bytes 6148
  1.5 1.0 %copy-start = (f32[5,2,64,128]{3,2,1,0:T(8,128)S(1)}, f32[5,2,64,128]{3,2,1,0:T(8,128)}, u32[]{:S(2)}) copy-start(f32[5,2,64,128]{3,2,1,0:T(8,128)} %param.4) | copy-start | bytes 983044
  2.5 0.9 %copy-start.1 = (f32[1,1,8,5,4,256]{5,4,3,2,1,0:T(4,128)S(1)}, f32[1,1,8,5,4,256]{5,4,3,2,1,0:T(4,128)}, u32[]{:S(2)}) copy-start(f32[1,1,8,5,4,256]{5,4,3,2,1,0:T(4,128)} %param.5) | copy-start | bytes 491524
where the time goes:
time: 62.8 us; the launch traced here: 62.6 us
  Pallas kernels  59.2 us (94%)
  local copies, waits for them, and re-layouts  2.75 us (4%)
  between operations  0.65 us (1%)
    pallas_call x1, Pallas kernels, body(): pl.pallas_call(functools.partial(level_kernel, n, m), out_shape=(shape((I...  44.8 us
    pallas_call x1, Pallas kernels, body(): pl.pallas_call(functools.partial(merge_kernel, n), out_shape=(shape((IMAG...  14.3 us
    unnamed x8, local copies, waits for them, and re-layouts  2.75 us

commit v1 on v0

--- a/solution.py
+++ b/solution.py
@@ -14,6 +14,7 @@
 IMAGES = 10
 ROWS = 64
 LANES = 128
+VMEM_LIMIT = 65280 * 1024
 
 
 def iota(shape, dim):
@@ -26,6 +27,19 @@
         if shift == 0:
             return x
     return pltpu.roll(x, shift, axis)
+
+
+def select_dot(values, weights):
+    x = jnp.concatenate(values, axis=0)
+    high = x.astype(jnp.bfloat16)
+    x = x - high.astype(jnp.float32)
+    middle = x.astype(jnp.bfloat16)
+    low = (x - middle.astype(jnp.float32)).astype(jnp.bfloat16)
+    weights = weights.astype(jnp.bfloat16)
+    parts = [
+        jnp.dot(part, weights, preferred_element_type=jnp.float32) for part in (low, middle, high)
+    ]
+    return parts[0] + parts[1] + parts[2]
 
 
 def primitives(u):
@@ -58,8 +72,7 @@
 
 
 def coarse_step(img, flux_x, flux_y):
-    first_row = iota((ROWS, LANES), 0) == 0
-    first_col = iota((ROWS, LANES), 1) == 0
+    row, col = iota((ROWS, LANES), 0), iota((ROWS, LANES), 1)
     cells, prims = [], []
     for z in range(2):
         u = [img[pl.ds((2 * f + z) * ROWS, ROWS), :] for f in range(5)]
@@ -70,14 +83,16 @@
     for z in range(2):
         u = cells[z]
         new = [u[f] - depth * (u[f] - cells[1 - z][f]) for f in range(5)]
-        for k, axis, first, saved in ((1, 0, first_row, flux_x), (2, 1, first_col, flux_y)):
+        for k, axis, place, saved in ((1, 0, row, flux_x), (2, 1, col, flux_y)):
             state = scaled_state(u, *prims[z], k)
             before = [roll(s, 1, axis) for s in state]
             faces = face_flux(before, state, k)
             for f in range(5):
-                face = jnp.where(first, 0.0, faces[f])
-                saved[pl.ds((2 * f + z) * ROWS, ROWS), :] = face
-                new[f] = new[f] - (roll(face, -1, axis) - face)
+                face = jnp.where(place == 0, 0.0, faces[f])
+                upper = roll(face, -1, axis)
+                signed = jnp.where(place % 8 == 7, -upper, face)
+                saved[pl.ds((2 * f + z) * ROWS, ROWS), :] = signed
+                new[f] = new[f] - (upper - face)
         for f in range(5):
             img[pl.ds((IMAGES + 2 * f + z) * ROWS, ROWS), :] = new[f]
 
@@ -99,11 +114,11 @@
 def wanted_tile(sources, tiles, o, me):
     tile = jnp.int32(0)
     for r in range(BOXES):
-        tile = jnp.where(sources[o, r] == me, tiles[o, r], tile)
+        tile = jnp.where(sources[r, o] == me, tiles[r, o], tile)
     return tile
 
 
-def pack_rims(n, me, sources, tiles, table_x, table_y, by_tile, rims):
+def pack_rims(n, me, sources, tiles, table_x, table_y, by_tile, rims, wanted):
     group = iota((8, LANES), 1) // 8
     for tx in range(1, 7):
         for ty in range(1, 15):
@@ -119,7 +134,9 @@
             by_tile[16 * tx + ty] = message
 
     def one(o, carry):
-        rims[o] = by_tile[jnp.maximum(wanted_tile(sources, tiles, o, me), 17)]
+        tile = wanted_tile(sources, tiles, o, me)
+        wanted[o] = tile
+        rims[o] = by_tile[jnp.maximum(tile, 17)]
         return carry
 
     lax.fori_loop(0, n, one, 0)
@@ -176,7 +193,7 @@
 
 def own_rims(me, sources, rims, held):
     for r in range(BOXES):
-        held[pl.ds(8 * r, 8), :] = rims[sources[me, r]]
+        held[pl.ds(8 * r, 8), :] = rims[sources[r, me]]
     by_row = [held[pl.ds(s, BOXES, stride=8), :] for s in range(8)]
     lane = iota((BOXES, LANES), 1)
 
@@ -206,12 +223,7 @@
         weights = jnp.where(chosen, 1.0, 0.0)
         old = sides[side][:IMAGES]
         mid = [0.5 * (x + y) for x, y in zip(old, sides[side][IMAGES:])]
-        ghosts = jnp.dot(
-            jnp.concatenate(old + mid, axis=0),
-            weights,
-            precision=lax.Precision.HIGHEST,
-            preferred_element_type=jnp.float32,
-        )
+        ghosts = select_dot(old + mid, weights)
         spread.append(
             [
                 [ghosts[(IMAGES * t + i) * 8 : (IMAGES * t + i) * 8 + 8] for i in range(IMAGES)]
@@ -255,41 +267,39 @@
 def pack_results(n, me, sources, u, edges, held, packed, results):
     cell, target = iota((256, LANES), 0), iota((256, LANES), 1)
     a, b = cell // 16, cell % 16
-    flipped, along = 7 - a // 2, b // 2
-    average = (target < 64) & (target // 8 == flipped) & (target % 8 == along)
-    rows = ((target // 8 == 8) & (a == 0) | (target // 8 == 9) & (a == 15)) & (target % 8 == along)
-    cols = ((target // 8 == 10) & (b == 0) | (target // 8 == 11) & (b == 15)) & (
-        target % 8 == flipped
-    )
+    row, lane = target // 16, target % 16
+    average = (row == a // 2) & (lane - 1 == b // 2)
+    low_col = (row == a // 2) & (lane == 0) & (b == 0)
+    high_col = (row == a // 2) & (lane == 9) & (b == 15)
+    low_row = (target == b // 2) & (a == 0)
+    high_row = (target == 8 + b // 2) & (a == 15)
+
+    def weights(low, high):
+        return jnp.where(low, -0.125, jnp.where(high, 0.125, 0.0))
+
     thick = [u[i // 2][2 * (i % 2)] + u[i // 2][2 * (i % 2) + 1] for i in range(IMAGES)]
-    total = None
-    for values, weights in ((thick, average), (edges[0], rows), (edges[1], cols)):
-        part = jnp.dot(
-            jnp.concatenate(values, axis=0),
-            jnp.where(weights, 0.125, 0.0),
-            precision=lax.Precision.HIGHEST,
-            preferred_element_type=jnp.float32,
-        )
-        total = part if total is None else total + part
-    sums = [total[8 * i : 8 * i + 8] for i in range(IMAGES)]
+    inner = select_dot(thick, jnp.where(average, 0.125, 0.0))
+    inner = inner + select_dot(edges[1], weights(low_col, high_col))
+    outer = select_dot(edges[0], weights(low_row, high_row))
+    inner = [inner[8 * i : 8 * i + 8] for i in range(IMAGES)]
+    outer = [outer[8 * i : 8 * i + 8] for i in range(IMAGES)]
     lane = iota((BOXES, LANES), 1)
-    for q in range(5):
-        row = jnp.where(lane < 64, sums[2 * q], roll(sums[2 * q + 1], 64, 1))
-        held[pl.ds(q, BOXES, stride=8), :] = row
-    for w in range(3):
-        row = jnp.zeros((BOXES, LANES), jnp.float32)
-        for h in range(4):
-            if 4 * w + h < IMAGES:
-                row = jnp.where(lane // 32 == h, roll(sums[4 * w + h], 32 * h - 64, 1), row)
-        held[pl.ds(5 + w, BOXES, stride=8), :] = row
-
+    for i in range(8):
+        message = roll(outer[i], 100, 1)
+        if i < 4:
+            last = roll(outer[8 + i % 2], 116 if i < 2 else 108, 1)
+            message = jnp.where(lane < 116, message, last)
+        for image in range(IMAGES - 1, -1, -1):
+            part = roll(inner[image], 10 * image - 16 * i, 1)
+            message = jnp.where(lane < 10 * image + 10, part, message)
+        held[pl.ds(i, BOXES, stride=8), :] = message
     for r in range(BOXES):
         packed[r] = held[pl.ds(8 * r, 8), :]
 
     def one(s, carry):
         box = jnp.int32(0)
         for r in range(BOXES):
-            box = jnp.where(sources[me, r] == s, r, box)
+            box = jnp.where(sources[r, me] == s, r, box)
         results[s] = packed[box]
         return carry
 
@@ -324,16 +334,19 @@
     n,
     m,
     coarse,
-    fine,
-    sources,
-    tiles,
+    fine_in,
+    sources_in,
+    tiles_in,
     coarse_new,
-    rows_x,
+    flux_x,
     flux_y,
     returned,
     fine_out,
+    wanted,
+    sources,
+    tiles,
     img,
-    flux_x,
+    fine,
     turned,
     table_x,
     table_y,
@@ -348,6 +361,7 @@
     halo_cols,
     from_rows,
     from_cols,
+    load_sems,
     rim_sems,
     result_sems,
     halo_sems,
@@ -366,12 +380,22 @@
     pl.semaphore_signal(barrier, 1, device_id={"gy": right}, device_id_type=MESH)
     pl.semaphore_signal(barrier, 1, device_id={"gy": left}, device_id_type=MESH)
 
-    img[pl.ds(0, IMAGES * ROWS), :] = coarse[...]
+    load = pltpu.make_async_copy(coarse, img.at[pl.ds(0, IMAGES * ROWS)], load_sems.at[0])
+    load_fine = pltpu.make_async_copy(fine_in, fine, load_sems.at[1])
+    load_sources = pltpu.make_async_copy(sources_in, sources, load_sems.at[2])
+    load_tiles = pltpu.make_async_copy(tiles_in, tiles, load_sems.at[3])
+    load.start()
+    load_sources.start()
+    load_tiles.start()
+    load_fine.start()
+    load.wait()
     coarse_step(img, flux_x, flux_y)
     table_x[...] = jnp.zeros_like(table_x)
     table_y[...] = jnp.zeros_like(table_y)
     build_tables(img, turned, table_x, table_y)
-    pack_rims(n, me, sources, tiles, table_x, table_y, by_tile, rims)
+    load_sources.wait()
+    load_tiles.wait()
+    pack_rims(n, me, sources, tiles, table_x, table_y, by_tile, rims, wanted)
     pack_halo(img, halo_rows, halo_cols)
     pl.semaphore_wait(barrier, n + 1)
 
@@ -395,14 +419,11 @@
         )
         copy.start()
         halos.append(copy)
+    load_fine.wait()
     for r in range(BOXES):
         for f in range(5):
             for z in range(4):
                 cells[4 * f + z, pl.ds(r, 1), :] = fine[r, f, pl.ds(z, 1), :]
-    for i in range(8):
-        for image in range(IMAGES):
-            rows_x[i, pl.ds(image, 1), :] = flux_x[pl.ds(image * ROWS + 8 * i, 1), :]
-    rows_x[:, pl.ds(IMAGES, 6), :] = jnp.zeros((8, 6, LANES), jnp.float32)
     for copy in halos:
         copy.wait_recv()
     finish_edges(img, halo_rows, halo_cols, from_rows, from_cols)
@@ -429,91 +450,112 @@
     result_copies.wait_send()
 
 
-def merge_kernel(n, new, rows_x, flux_y, returned, sources, tiles, fine, out, fine_out):
-    me = lax.axis_index("gx")
-    out[...] = new[...]
+def merge_kernel(
+    n, new, flux_x, flux_y, returned, wanted, fine, out, fine_out, slots, marks, outer, inner
+):
     fine_out[...] = fine[...]
     lane, sub = iota((8, LANES), 1), iota((8, LANES), 0)
 
-    def spread(o, row):
-        return jnp.broadcast_to(returned[o, pl.ds(row, 1), :], (8, LANES))
-
-    def turned(x, shift, stride):
-        x = pltpu.roll(x, 0, 1, stride=stride, stride_axis=0)
-        return pltpu.roll(x, lax.rem(shift + 2 * LANES, LANES), 1)
-
-    def correct(o, carry):
-        tile = wanted_tile(sources, tiles, o, me)
-
-        @pl.when(tile > 0)
-        def _():
-            tx, ty = tile // 16, tile % 16
-            inside = lane // 8 == ty
-            low_face = rows_x[tx]
-            high_face = rows_x[tx + 1]
+    def clear(t, carry):
+        slots[t] = -1
+        return carry
+
+    def place(o, carry):
+        slots[wanted[o]] = o
+        return carry
+
+    lax.fori_loop(0, 128, clear, 0, unroll=8)
+    lax.fori_loop(0, n, place, 0, unroll=8)
+    blank = jnp.zeros((8, LANES), jnp.float32)
+    for tx in (0, 7):
+        for i in range(2):
+            marks[tx, i] = blank
+        for image in range(IMAGES):
+            inner[tx, image] = blank
+        for g in range(3):
+            outer[tx, g] = blank
+
+    def row_of_tiles(tx, carry):
+        parts = [blank] * IMAGES
+        sides = [blank] * 3
+        covered, touched = blank, blank
+        before = jnp.int32(0)
+        for ty in range(1, 15):
+            slot = slots[16 * tx + ty]
+            live = (slot >= 0).astype(jnp.int32)
+            message = returned[jnp.maximum(slot, 0)]
+            here = (lane // 8 == ty) & (lane < 1024 * live)
+            first = jnp.where(live > 0, 8 * ty - 1 + before, 1024)
+            wide = (lane >= first) & (lane < 8 * ty + 9)
+            covered = jnp.where(here, 1.0, covered)
+            touched = jnp.where(wide, 1.0, touched)
             for image in range(IMAGES):
-                base = 32 * (image % 4)
-                values = spread(o, 5 + image // 4)
-                here = image * ROWS + 8 * tx
-                rows = pl.ds(pl.multiple_of(here - 8, 8), 8)
-                low = pltpu.roll(values, lax.rem(8 * ty - base + LANES, LANES), 1)
-                change = low - low_face[image : image + 1]
-                out[rows, :] = out[rows, :] - jnp.where(inside & (sub == 7), change, 0.0)
-                rows = pl.ds(pl.multiple_of(here + 8, 8), 8)
-                high = pltpu.roll(values, lax.rem(8 * ty - base - 8 + 2 * LANES, LANES), 1)
-                change = high - high_face[image : image + 1]
-                out[rows, :] = out[rows, :] + jnp.where(inside & (sub == 0), change, 0.0)
-                rows = pl.ds(pl.multiple_of(here, 8), 8)
-                faces = flux_y[rows, :]
-                low = turned(values, 8 * ty - 1 - base - 23, 1) - pltpu.roll(faces, LANES - 1, 1)
-                high = turned(values, 8 * ty + 8 - base - 31, 1) - faces
-                change = jnp.where(lane == 8 * ty + 8, high, 0.0)
-                change = jnp.where(lane == 8 * ty - 1, -low, change)
-                out[rows, :] = out[rows, :] + change
-
-        return carry
-
-    def average(o, carry):
-        tile = wanted_tile(sources, tiles, o, me)
-
-        @pl.when(tile > 0)
-        def _():
-            tx, ty = tile // 16, tile % 16
-            inside = lane // 8 == ty
-            for image in range(IMAGES):
-                rows = pl.ds(pl.multiple_of(image * ROWS + 8 * tx, 8), 8)
-                values = turned(spread(o, image // 2), 8 * ty - 64 * (image % 2) - 56, 8)
-                out[rows, :] = jnp.where(inside, values, out[rows, :])
-
-        return carry
-
-    lax.fori_loop(0, n, correct, 0)
-    lax.fori_loop(0, n, average, 0)
+                turned = roll(message, 8 * ty - 1 - 10 * image, 1)
+                parts[image] = jnp.where(wide, turned, parts[image])
+            for g in range(3):
+                sides[g] = jnp.where(here, roll(message, 8 * ty - 100 - 8 * g, 1), sides[g])
+            before = live
+        marks[tx, 0] = covered
+        marks[tx, 1] = touched
+        for image in range(IMAGES):
+            inner[tx, image] = parts[image]
+        for g in range(3):
+            outer[tx, g] = sides[g]
+        return carry
+
+    lax.fori_loop(1, 7, row_of_tiles, 0)
+
+    def finish(tx, carry):
+        above, below = jnp.minimum(tx + 1, 7), jnp.maximum(tx - 1, 0)
+        covered = marks[tx, 0] > 0.5
+        touched = marks[tx, 1] > 0.5
+        beside = (sub == 7) & (marks[above, 0] > 0.5) | (sub == 0) & (marks[below, 0] > 0.5)
+        low, high = [outer[above, g] for g in range(3)], [outer[below, g] for g in range(3)]
+        for image in range(IMAGES):
+            if image < 8:
+                lows, highs = low[0][image : image + 1], high[1][image : image + 1]
+            else:
+                lows, highs = low[2][image - 8 : image - 7], high[2][image - 6 : image - 5]
+            rows = pl.ds(pl.multiple_of(image * ROWS + 8 * tx, 8), 8)
+            value = inner[tx, image]
+            cells = new[rows, :] + jnp.where(touched, value - flux_y[rows, :], 0.0)
+            faces = jnp.where(sub == 7, lows, highs)
+            cells = cells + jnp.where(beside, faces - flux_x[rows, :], 0.0)
+            out[rows, :] = jnp.where(covered, value, cells)
+        return carry
+
+    lax.fori_loop(0, 8, finish, 0)
 
 
 def body(n, m, coarse_state, fine_state, source_rows, tile_ids):
     vmem = pl.BlockSpec(memory_space=pltpu.VMEM)
     smem = pl.BlockSpec(memory_space=pltpu.SMEM)
+    hbm = pl.BlockSpec(memory_space=pltpu.HBM)
     f32 = jnp.float32
     coarse = coarse_state.reshape(IMAGES * ROWS, LANES)
     fine = fine_state.reshape(BOXES, 5, 4, 256)
-    sources = source_rows.reshape(n, BOXES)
-    tiles = tile_ids.reshape(n, BOXES)
+    sources = source_rows.reshape(n, BOXES).T
+    tiles = tile_ids.reshape(n, BOXES).T
     shape = jax.ShapeDtypeStruct
-    new, rows_x, flux_y, returned, fine_out = pl.pallas_call(
+    image = shape((IMAGES * ROWS, LANES), f32)
+    boxes = shape((BOXES, 5, 4, 256), f32)
+    new, flux_x, flux_y, returned, fine_out, wanted = pl.pallas_call(
         functools.partial(level_kernel, n, m),
         out_shape=(
-            shape((IMAGES * ROWS, LANES), f32),
-            shape((8, 16, LANES), f32),
-            shape((IMAGES * ROWS, LANES), f32),
+            image,
+            image,
+            image,
             shape((n, 8, LANES), f32),
-            shape((BOXES, 5, 4, 256), f32),
+            boxes,
+            shape((n,), jnp.int32),
         ),
-        in_specs=[vmem, vmem, smem, smem],
-        out_specs=(vmem,) * 5,
+        in_specs=[hbm] * 4,
+        out_specs=(vmem,) * 5 + (smem,),
         scratch_shapes=[
+            pltpu.SMEM((BOXES, n), jnp.int32),
+            pltpu.SMEM((BOXES, n), jnp.int32),
             pltpu.VMEM((2 * IMAGES * ROWS, LANES), f32),
-            pltpu.VMEM((IMAGES * ROWS, LANES), f32),
+            pltpu.VMEM((BOXES, 5, 4, 256), f32),
             pltpu.VMEM((IMAGES * LANES, LANES), f32),
             pltpu.VMEM((8, 40, LANES), f32),
             pltpu.VMEM((16, 24, LANES), f32),
@@ -528,26 +570,30 @@
             pltpu.VMEM((ROWS, LANES), f32),
             pltpu.VMEM((2, 32, LANES), f32),
             pltpu.VMEM((2, ROWS, LANES), f32),
+            pltpu.SemaphoreType.DMA((4,)),
             pltpu.SemaphoreType.DMA((2,)),
             pltpu.SemaphoreType.DMA((2,)),
             pltpu.SemaphoreType.DMA((2, 4)),
         ],
         compiler_params=pltpu.CompilerParams(
-            collective_id=0, has_side_effects=True, vmem_limit_bytes=40 * 1024 * 1024
+            collective_id=0, has_side_effects=True, vmem_limit_bytes=VMEM_LIMIT
         ),
         name="levels",
     )(coarse, fine, sources, tiles)
     out, fine_out = pl.pallas_call(
         functools.partial(merge_kernel, n),
-        out_shape=(
-            shape((IMAGES * ROWS, LANES), f32),
-            shape((BOXES, 5, 4, 256), f32),
-        ),
-        in_specs=[vmem, vmem, vmem, vmem, smem, smem, vmem],
+        out_shape=(image, boxes),
+        in_specs=[vmem, vmem, vmem, vmem, smem, vmem],
         out_specs=(vmem,) * 2,
-        compiler_params=pltpu.CompilerParams(vmem_limit_bytes=40 * 1024 * 1024),
+        scratch_shapes=[
+            pltpu.SMEM((128,), jnp.int32),
+            pltpu.VMEM((8, 2, 8, LANES), f32),
+            pltpu.VMEM((8, 3, 8, LANES), f32),
+            pltpu.VMEM((8, IMAGES, 8, LANES), f32),
+        ],
+        compiler_params=pltpu.CompilerParams(vmem_limit_bytes=VMEM_LIMIT),
         name="merge",
-    )(new, rows_x, flux_y, returned, sources, tiles, fine_out)
+    )(new, flux_x, flux_y, returned, wanted, fine_out)
     return out.reshape(coarse_state.shape), fine_out.reshape(fine_state.shape)
 
 

time: 62.8 us -> 49.6 us (0.79)
  the two profiles are of different devices: /device:TPU:2 before, /device:TPU:14 now
where the time goes in v1:
time: 49.6 us; the launch traced here: 49.4 us
  Pallas kernels  48.8 us (98%)
  between operations  0.64 us (1%)
    pallas_call x1, Pallas kernels, body(): pl.pallas_call(functools.partial(level_kernel, n, m), out_shape=(image, i...  44.6 us
    pallas_call x1, Pallas kernels, body(): pl.pallas_call(functools.partial(merge_kernel, n), out_shape=(image, boxe...  4.18 us

profile of v1, /device:TPU:14, one launch (start us, length us, event | category | flops | bytes accessed | tf_op | source)
XLA Modules:
  0.0 49.4 jit_solution(17576885381504451021)
XLA Ops:
  0.6 44.6 %levels.1 = (f32[640,128]{1,0:T(8,128)}, f32[640,128]{1,0:T(8,128)}, f32[640,128]{1,0:T(8,128)}, f32[64,8,128]{2,1,0:T(8,128)}, f32[8,5,4,256]{3,2,1,0:T(4,128)}, /*index=5*/s32[64]{0:T(128)}) custom-call(f32[640,128]{1,0:T(8,128)} %bitcast.10, f32[8,5,4,256]{3,2,1,0:T(4,128)} %bitcast.11, s32[8,64]{1,0:T(8,128)} %bitcast.12, s32[8,64]{1,0:T(8,128)} %bitcast.13), custom_call_target="tpu_custom_call" | custom-call | tf_op jit(solution)/shard_map/levels/pallas_call | solution.py:542
  45.2 4.2 %merge.1 = (f32[640,128]{1,0:T(8,128)}, f32[8,5,4,256]{3,2,1,0:T(4,128)}) custom-call(f32[640,128]{1,0:T(8,128)} %get-tuple-element.10.new, f32[640,128]{1,0:T(8,128)} %get-tuple-element.11.flux_x, f32[640,128]{1,0:T(8,128)} %get-tuple-element.12.flux_y, f32[64,8,128]{2,1,0:T(8,128)} %get-tuple-element.13.returned, s32[64]{0:T(128)} %get-tuple-element.14.wanted, ...), custom_call_target="tpu_custom_call" | custom-call | tf_op jit(solution)/shard_map/merge/pallas_call | solution.py:583

commit v2 on v1

--- a/solution.py
+++ b/solution.py
@@ -35,7 +35,6 @@
     x = x - high.astype(jnp.float32)
     middle = x.astype(jnp.bfloat16)
     low = (x - middle.astype(jnp.float32)).astype(jnp.bfloat16)
-    weights = weights.astype(jnp.bfloat16)
     parts = [
         jnp.dot(part, weights, preferred_element_type=jnp.float32) for part in (low, middle, high)
     ]
@@ -118,7 +117,7 @@
     return tile
 
 
-def pack_rims(n, me, sources, tiles, table_x, table_y, by_tile, rims, wanted):
+def pack_rims(n, me, sources, tiles, table_x, table_y, by_tile, rims, wanted, box_of):
     group = iota((8, LANES), 1) // 8
     for tx in range(1, 7):
         for ty in range(1, 15):
@@ -137,6 +136,10 @@
         tile = wanted_tile(sources, tiles, o, me)
         wanted[o] = tile
         rims[o] = by_tile[jnp.maximum(tile, 17)]
+        box = jnp.int32(0)
+        for r in range(BOXES):
+            box = jnp.where(sources[r, me] == o, r, box)
+        box_of[o] = box
         return carry
 
     lax.fori_loop(0, n, one, 0)
@@ -191,7 +194,31 @@
             img[rows, :] = cells
 
 
-def own_rims(me, sources, rims, held):
+def spread_weights(weights):
+    source, cell = iota((LANES, 256), 0), iota((LANES, 256), 1)
+    a, b = cell // 16, cell % 16
+    for side, (along, across) in enumerate(((b, a), (a, b))):
+        chosen = (source < 16) & (source % 8 == along // 2) & (source // 8 == across // 8)
+        weights[side] = jnp.where(chosen, 1.0, 0.0).astype(jnp.bfloat16)
+
+
+def gather_weights(weights):
+    cell, target = iota((256, LANES), 0), iota((256, LANES), 1)
+    a, b = cell // 16, cell % 16
+    row, lane = target // 16, target % 16
+    average = (row == a // 2) & (lane - 1 == b // 2)
+    low_col = (row == a // 2) & (lane == 0) & (b == 0)
+    high_col = (row == a // 2) & (lane == 9) & (b == 15)
+    low_row = (target == b // 2) & (a == 0)
+    high_row = (target == 8 + b // 2) & (a == 15)
+    for i, (low, high) in enumerate(((None, average), (low_col, high_col), (low_row, high_row))):
+        values = jnp.where(high, 0.125, 0.0)
+        if low is not None:
+            values = jnp.where(low, -0.125, values)
+        weights[i] = values.astype(jnp.bfloat16)
+
+
+def own_rims(me, sources, rims, held, weights):
     for r in range(BOXES):
         held[pl.ds(8 * r, 8), :] = rims[sources[r, me]]
     by_row = [held[pl.ds(s, BOXES, stride=8), :] for s in range(8)]
@@ -215,15 +242,11 @@
         else:
             sides[1].append(pair(by_row[p - 8], 96 + 8 * j, by_row[p - 6], 96 + 8 * j))
 
-    source, cell = iota((LANES, 256), 0), iota((LANES, 256), 1)
-    a, b = cell // 16, cell % 16
     spread = []
-    for side, (along, across) in enumerate(((b, a), (a, b))):
-        chosen = (source < 16) & (source % 8 == along // 2) & (source // 8 == across // 8)
-        weights = jnp.where(chosen, 1.0, 0.0)
+    for side in range(2):
         old = sides[side][:IMAGES]
         mid = [0.5 * (x + y) for x, y in zip(old, sides[side][IMAGES:])]
-        ghosts = select_dot(old + mid, weights)
+        ghosts = select_dot(old + mid, weights[side])
         spread.append(
             [
                 [ghosts[(IMAGES * t + i) * 8 : (IMAGES * t + i) * 8 + 8] for i in range(IMAGES)]
@@ -264,23 +287,11 @@
     return new
 
 
-def pack_results(n, me, sources, u, edges, held, packed, results):
-    cell, target = iota((256, LANES), 0), iota((256, LANES), 1)
-    a, b = cell // 16, cell % 16
-    row, lane = target // 16, target % 16
-    average = (row == a // 2) & (lane - 1 == b // 2)
-    low_col = (row == a // 2) & (lane == 0) & (b == 0)
-    high_col = (row == a // 2) & (lane == 9) & (b == 15)
-    low_row = (target == b // 2) & (a == 0)
-    high_row = (target == 8 + b // 2) & (a == 15)
-
-    def weights(low, high):
-        return jnp.where(low, -0.125, jnp.where(high, 0.125, 0.0))
-
+def pack_results(u, edges, weights, held, packed):
     thick = [u[i // 2][2 * (i % 2)] + u[i // 2][2 * (i % 2) + 1] for i in range(IMAGES)]
-    inner = select_dot(thick, jnp.where(average, 0.125, 0.0))
-    inner = inner + select_dot(edges[1], weights(low_col, high_col))
-    outer = select_dot(edges[0], weights(low_row, high_row))
+    inner = select_dot(thick, weights[0])
+    inner = inner + select_dot(edges[1], weights[1])
+    outer = select_dot(edges[0], weights[2])
     inner = [inner[8 * i : 8 * i + 8] for i in range(IMAGES)]
     outer = [outer[8 * i : 8 * i + 8] for i in range(IMAGES)]
     lane = iota((BOXES, LANES), 1)
@@ -296,30 +307,32 @@
     for r in range(BOXES):
         packed[r] = held[pl.ds(8 * r, 8), :]
 
-    def one(s, carry):
-        box = jnp.int32(0)
-        for r in range(BOXES):
-            box = jnp.where(sources[r, me] == s, r, box)
-        results[s] = packed[box]
-        return carry
-
-    lax.fori_loop(0, n, one, 0)
-
-
-def exchange(n, me, source, target, sems):
-    def send(step, carry):
-        other = lax.rem(me + step, n)
-        pltpu.make_async_remote_copy(
-            src_ref=source.at[other],
-            dst_ref=target.at[me],
-            send_sem=sems.at[0],
-            recv_sem=sems.at[1],
-            device_id={"gx": other},
-            device_id_type=MESH,
-        ).start()
-        return carry
-
-    lax.fori_loop(1, n, send, 0)
+
+def far_first(n):
+    side = round(n**0.5)
+    steps = [(a, b) for a in range(side) for b in range(side) if a or b]
+    return side, sorted(steps, key=lambda s: -sum(min(x, side - x) for x in s))
+
+
+def partners(n, me):
+    side, steps = far_first(n)
+    high, low = me // side, lax.rem(me, side)
+    for a, b in steps:
+        yield lax.rem(high + a, side) * side + lax.rem(low + b, side)
+
+
+def send(me, other, source, target, sems):
+    pltpu.make_async_remote_copy(
+        src_ref=source.at[other],
+        dst_ref=target.at[me],
+        send_sem=sems.at[0],
+        recv_sem=sems.at[1],
+        device_id={"gx": other},
+        device_id_type=MESH,
+    ).start()
+
+
+def all_slots(n, me, source, target, sems):
     return pltpu.make_async_remote_copy(
         src_ref=source.at[pl.ds(0, n - 1)],
         dst_ref=target.at[pl.ds(0, n - 1)],
@@ -338,14 +351,18 @@
     sources_in,
     tiles_in,
     coarse_new,
+    flux_x_out,
+    flux_y_out,
+    returned,
+    fine_out,
+    wanted_out,
+    sources,
+    tiles,
+    wanted,
+    box_of,
+    img,
     flux_x,
     flux_y,
-    returned,
-    fine_out,
-    wanted,
-    sources,
-    tiles,
-    img,
     fine,
     turned,
     table_x,
@@ -361,7 +378,10 @@
     halo_cols,
     from_rows,
     from_cols,
+    spread,
+    gather,
     load_sems,
+    store_sems,
     rim_sems,
     result_sems,
     halo_sems,
@@ -371,16 +391,13 @@
     right, left = lax.rem(column + 1, m), lax.rem(column + m - 1, m)
     barrier = pltpu.get_barrier_semaphore()
 
-    def greet(step, carry):
-        other = lax.rem(me + step, n)
+    for other in partners(n, me):
         pl.semaphore_signal(barrier, 1, device_id={"gx": other}, device_id_type=MESH)
-        return carry
-
-    lax.fori_loop(1, n, greet, 0)
     pl.semaphore_signal(barrier, 1, device_id={"gy": right}, device_id_type=MESH)
     pl.semaphore_signal(barrier, 1, device_id={"gy": left}, device_id_type=MESH)
 
-    load = pltpu.make_async_copy(coarse, img.at[pl.ds(0, IMAGES * ROWS)], load_sems.at[0])
+    old, new = pl.ds(0, IMAGES * ROWS), pl.ds(IMAGES * ROWS, IMAGES * ROWS)
+    load = pltpu.make_async_copy(coarse, img.at[old], load_sems.at[0])
     load_fine = pltpu.make_async_copy(fine_in, fine, load_sems.at[1])
     load_sources = pltpu.make_async_copy(sources_in, sources, load_sems.at[2])
     load_tiles = pltpu.make_async_copy(tiles_in, tiles, load_sems.at[3])
@@ -390,16 +407,33 @@
     load_fine.start()
     load.wait()
     coarse_step(img, flux_x, flux_y)
+    stores = [
+        pltpu.make_async_copy(flux_x, flux_x_out, store_sems.at[0]),
+        pltpu.make_async_copy(flux_y, flux_y_out, store_sems.at[1]),
+    ]
+    stores[0].start()
+    stores[1].start()
     table_x[...] = jnp.zeros_like(table_x)
     table_y[...] = jnp.zeros_like(table_y)
     build_tables(img, turned, table_x, table_y)
     load_sources.wait()
     load_tiles.wait()
-    pack_rims(n, me, sources, tiles, table_x, table_y, by_tile, rims, wanted)
+    pack_rims(n, me, sources, tiles, table_x, table_y, by_tile, rims, wanted, box_of)
+    rims_in[me] = rims[me]
+    stores.append(pltpu.make_async_copy(wanted, wanted_out, store_sems.at[2]))
+    stores[2].start()
     pack_halo(img, halo_rows, halo_cols)
+    load_fine.wait()
+    for r in range(BOXES):
+        for f in range(5):
+            for z in range(4):
+                cells[4 * f + z, pl.ds(r, 1), :] = fine[r, f, pl.ds(z, 1), :]
+    spread_weights(spread)
+    gather_weights(gather)
     pl.semaphore_wait(barrier, n + 1)
 
-    rim_copies = exchange(n, me, rims, rims_in, rim_sems)
+    for other in partners(n, me):
+        send(me, other, rims, rims_in, rim_sems)
     halos = []
     for i, (source, target, where) in enumerate(
         (
@@ -419,41 +453,76 @@
         )
         copy.start()
         halos.append(copy)
-    load_fine.wait()
-    for r in range(BOXES):
-        for f in range(5):
-            for z in range(4):
-                cells[4 * f + z, pl.ds(r, 1), :] = fine[r, f, pl.ds(z, 1), :]
-    for copy in halos:
-        copy.wait_recv()
-    finish_edges(img, halo_rows, halo_cols, from_rows, from_cols)
-    coarse_new[...] = img[pl.ds(IMAGES * ROWS, IMAGES * ROWS), :]
-
+
+    rim_copies = all_slots(n, me, rims, rims_in, rim_sems)
     rim_copies.wait_recv()
-    rims_in[me] = rims[me]
-    ghosts = own_rims(me, sources, rims_in, held)
+    ghosts = own_rims(me, sources, rims_in, held, spread)
     u = [[cells[4 * f + z] for z in range(4)] for f in range(5)]
     edges = [[None] * IMAGES, [None] * IMAGES]
     u = fine_step(u, ghosts[0][0], ghosts[1][0], edges)
     u = fine_step(u, ghosts[0][1], ghosts[1][1], edges)
-    pack_results(n, me, sources, u, edges, held, packed, results)
-    result_copies = exchange(n, me, results, returned, result_sems)
+    pack_results(u, edges, gather, held, packed)
+    for other in partners(n, me):
+        results[other] = packed[box_of[other]]
+        send(me, other, results, returned, result_sems)
+    results[me] = packed[box_of[me]]
+    stores.append(pltpu.make_async_copy(results.at[me], returned.at[me], store_sems.at[3]))
+    stores[3].start()
     for f in range(5):
         for z in range(4):
             for r in range(BOXES):
-                fine_out[r, f, pl.ds(z, 1), :] = u[f][z][r : r + 1]
+                fine[r, f, pl.ds(z, 1), :] = u[f][z][r : r + 1]
+    stores.append(pltpu.make_async_copy(fine, fine_out, store_sems.at[4]))
+    stores[4].start()
+    for copy in halos:
+        copy.wait_recv()
+    finish_edges(img, halo_rows, halo_cols, from_rows, from_cols)
+    stores.append(pltpu.make_async_copy(img.at[new], coarse_new, store_sems.at[5]))
+    stores[5].start()
     rim_copies.wait_send()
     for copy in halos:
         copy.wait_send()
+    for copy in stores:
+        copy.wait()
+    result_copies = all_slots(n, me, results, returned, result_sems)
+    result_copies.wait_send()
     result_copies.wait_recv()
-    returned[me] = results[me]
-    result_copies.wait_send()
 
 
 def merge_kernel(
-    n, new, flux_x, flux_y, returned, wanted, fine, out, fine_out, slots, marks, outer, inner
+    n,
+    new_in,
+    flux_x_in,
+    flux_y_in,
+    returned_in,
+    wanted_in,
+    fine_in,
+    out_to,
+    fine_out,
+    new,
+    flux_x,
+    flux_y,
+    returned,
+    wanted,
+    out,
+    slots,
+    marks,
+    outer,
+    inner,
+    sems,
+    out_sem,
 ):
-    fine_out[...] = fine[...]
+    pairs = (
+        (wanted_in, wanted),
+        (returned_in, returned),
+        (new_in, new),
+        (flux_x_in, flux_x),
+        (flux_y_in, flux_y),
+        (fine_in, fine_out),
+    )
+    loads = [pltpu.make_async_copy(a, b, sems.at[i]) for i, (a, b) in enumerate(pairs)]
+    for copy in loads:
+        copy.start()
     lane, sub = iota((8, LANES), 1), iota((8, LANES), 0)
 
     def clear(t, carry):
@@ -465,6 +534,7 @@
         return carry
 
     lax.fori_loop(0, 128, clear, 0, unroll=8)
+    loads[0].wait()
     lax.fori_loop(0, n, place, 0, unroll=8)
     blank = jnp.zeros((8, LANES), jnp.float32)
     for tx in (0, 7):
@@ -503,33 +573,37 @@
             outer[tx, g] = sides[g]
         return carry
 
+    loads[1].wait()
     lax.fori_loop(1, 7, row_of_tiles, 0)
+    for copy in loads[2:5]:
+        copy.wait()
 
     def finish(tx, carry):
         above, below = jnp.minimum(tx + 1, 7), jnp.maximum(tx - 1, 0)
         covered = marks[tx, 0] > 0.5
         touched = marks[tx, 1] > 0.5
         beside = (sub == 7) & (marks[above, 0] > 0.5) | (sub == 0) & (marks[below, 0] > 0.5)
+        rows = pl.ds(pl.multiple_of(8 * tx, 8), 8)
         low, high = [outer[above, g] for g in range(3)], [outer[below, g] for g in range(3)]
         for image in range(IMAGES):
             if image < 8:
                 lows, highs = low[0][image : image + 1], high[1][image : image + 1]
             else:
                 lows, highs = low[2][image - 8 : image - 7], high[2][image - 6 : image - 5]
-            rows = pl.ds(pl.multiple_of(image * ROWS + 8 * tx, 8), 8)
             value = inner[tx, image]
-            cells = new[rows, :] + jnp.where(touched, value - flux_y[rows, :], 0.0)
+            cells = new[image, rows, :] + jnp.where(touched, value - flux_y[image, rows, :], 0.0)
             faces = jnp.where(sub == 7, lows, highs)
-            cells = cells + jnp.where(beside, faces - flux_x[rows, :], 0.0)
-            out[rows, :] = jnp.where(covered, value, cells)
+            cells = cells + jnp.where(beside, faces - flux_x[image, rows, :], 0.0)
+            out[image, rows, :] = jnp.where(covered, value, cells)
+        pltpu.make_async_copy(out.at[:, rows], out_to.at[:, rows], out_sem).start()
         return carry
 
     lax.fori_loop(0, 8, finish, 0)
+    pltpu.make_async_copy(out, out_to, out_sem).wait()
+    loads[5].wait()
 
 
 def body(n, m, coarse_state, fine_state, source_rows, tile_ids):
-    vmem = pl.BlockSpec(memory_space=pltpu.VMEM)
-    smem = pl.BlockSpec(memory_space=pltpu.SMEM)
     hbm = pl.BlockSpec(memory_space=pltpu.HBM)
     f32 = jnp.float32
     coarse = coarse_state.reshape(IMAGES * ROWS, LANES)
@@ -550,11 +624,15 @@
             shape((n,), jnp.int32),
         ),
         in_specs=[hbm] * 4,
-        out_specs=(vmem,) * 5 + (smem,),
+        out_specs=(hbm,) * 6,
         scratch_shapes=[
             pltpu.SMEM((BOXES, n), jnp.int32),
             pltpu.SMEM((BOXES, n), jnp.int32),
+            pltpu.SMEM((n,), jnp.int32),
+            pltpu.SMEM((n,), jnp.int32),
             pltpu.VMEM((2 * IMAGES * ROWS, LANES), f32),
+            pltpu.VMEM((IMAGES * ROWS, LANES), f32),
+            pltpu.VMEM((IMAGES * ROWS, LANES), f32),
             pltpu.VMEM((BOXES, 5, 4, 256), f32),
             pltpu.VMEM((IMAGES * LANES, LANES), f32),
             pltpu.VMEM((8, 40, LANES), f32),
@@ -570,7 +648,10 @@
             pltpu.VMEM((ROWS, LANES), f32),
             pltpu.VMEM((2, 32, LANES), f32),
             pltpu.VMEM((2, ROWS, LANES), f32),
+            pltpu.VMEM((2, LANES, 256), jnp.bfloat16),
+            pltpu.VMEM((3, 256, LANES), jnp.bfloat16),
             pltpu.SemaphoreType.DMA((4,)),
+            pltpu.SemaphoreType.DMA((6,)),
             pltpu.SemaphoreType.DMA((2,)),
             pltpu.SemaphoreType.DMA((2,)),
             pltpu.SemaphoreType.DMA((2, 4)),
@@ -580,20 +661,37 @@
         ),
         name="levels",
     )(coarse, fine, sources, tiles)
+    stack = shape((IMAGES, ROWS, LANES), f32)
+    field = pltpu.VMEM((IMAGES, ROWS, LANES), f32)
     out, fine_out = pl.pallas_call(
         functools.partial(merge_kernel, n),
-        out_shape=(image, boxes),
-        in_specs=[vmem, vmem, vmem, vmem, smem, vmem],
-        out_specs=(vmem,) * 2,
+        out_shape=(stack, boxes),
+        in_specs=[hbm] * 6,
+        out_specs=(hbm,) * 2,
         scratch_shapes=[
+            field,
+            field,
+            field,
+            pltpu.VMEM((n, 8, LANES), f32),
+            pltpu.SMEM((n,), jnp.int32),
+            field,
             pltpu.SMEM((128,), jnp.int32),
             pltpu.VMEM((8, 2, 8, LANES), f32),
             pltpu.VMEM((8, 3, 8, LANES), f32),
             pltpu.VMEM((8, IMAGES, 8, LANES), f32),
+            pltpu.SemaphoreType.DMA((6,)),
+            pltpu.SemaphoreType.DMA,
         ],
         compiler_params=pltpu.CompilerParams(vmem_limit_bytes=VMEM_LIMIT),
         name="merge",
-    )(new, flux_x, flux_y, returned, wanted, fine_out)
+    )(
+        new.reshape(stack.shape),
+        flux_x.reshape(stack.shape),
+        flux_y.reshape(stack.shape),
+        returned,
+        wanted,
+        fine_out,
+    )
     return out.reshape(coarse_state.shape), fine_out.reshape(fine_state.shape)
 
 

time: 49.6 us -> 48.7 us (0.982)
  Pallas kernels: 48.8 us -> 47.9 us
    pallas_call x1, Pallas kernels: 44.6 us -> 41.8 us  [body(): pl.pallas_call(functools.partial(level_kernel, n, m), out_shape=(image, i...]
    pallas_call x1, Pallas kernels: 4.18 us -> 6.14 us  [body(): pl.pallas_call(functools.partial(merge_kernel, n), out_shape=(stack, boxe...]
where the time goes in v2:
time: 48.7 us; the launch traced here: 48.6 us
  Pallas kernels  47.9 us (98%)
  between operations  0.64 us (1%)
    pallas_call x1, Pallas kernels, body(): pl.pallas_call(functools.partial(level_kernel, n, m), out_shape=(image, i...  41.8 us
    pallas_call x1, Pallas kernels, body(): pl.pallas_call(functools.partial(merge_kernel, n), out_shape=(stack, boxe...  6.14 us

profile of v2, /device:TPU:14, one launch (start us, length us, event | category | flops | bytes accessed | tf_op | source)
XLA Modules:
  0.0 48.6 jit_solution(16730205182139532290)
XLA Ops:
  0.6 41.8 %levels.1 = (f32[640,128]{1,0:T(8,128)}, f32[640,128]{1,0:T(8,128)}, f32[640,128]{1,0:T(8,128)}, f32[64,8,128]{2,1,0:T(8,128)}, f32[8,5,4,256]{3,2,1,0:T(4,128)}, /*index=5*/s32[64]{0:T(128)}) custom-call(f32[640,128]{1,0:T(8,128)} %bitcast.16, f32[8,5,4,256]{3,2,1,0:T(4,128)} %bitcast.17, s32[8,64]{1,0:T(8,128)} %bitcast.18, s32[8,64]{1,0:T(8,128)} %bitcast.19), custom_call_target="tpu_custom_call" | custom-call | tf_op jit(solution)/shard_map/levels/pallas_call | solution.py:616
  42.4 6.1 %merge.1 = (f32[10,64,128]{2,1,0:T(8,128)}, f32[8,5,4,256]{3,2,1,0:T(4,128)}) custom-call(f32[10,64,128]{2,1,0:T(8,128)} %bitcast.13, f32[10,64,128]{2,1,0:T(8,128)} %bitcast.14, f32[10,64,128]{2,1,0:T(8,128)} %bitcast.15, f32[64,8,128]{2,1,0:T(8,128)} %get-tuple-element.13.returned_in, s32[64]{0:T(128)} %get-tuple-element.14.wanted_in, ...), custom_call_target="tpu_custom_call" | custom-call | tf_op jit(solution)/shard_map/merge/pallas_call | solution.py:666

commit v3 on v2

--- a/solution.py
+++ b/solution.py
@@ -203,14 +203,15 @@
 
 
 def gather_weights(weights):
-    cell, target = iota((256, LANES), 0), iota((256, LANES), 1)
+    source, target = iota((512, LANES), 0), iota((512, LANES), 1)
+    cell, half = source % 256, source // 256
     a, b = cell // 16, cell % 16
-    row, lane = target // 16, target % 16
-    average = (row == a // 2) & (lane - 1 == b // 2)
-    low_col = (row == a // 2) & (lane == 0) & (b == 0)
-    high_col = (row == a // 2) & (lane == 9) & (b == 15)
-    low_row = (target == b // 2) & (a == 0)
-    high_row = (target == 8 + b // 2) & (a == 15)
+    row, lane = target // 16 == a // 2, target % 16
+    average = row & (lane == 8 * half + b // 2)
+    low_col = row & (lane == 2 * half) & (b == 0)
+    high_col = row & (lane == 2 * half + 1) & (b == 15)
+    low_row = (target == 16 * half + b // 2) & (a == 0)
+    high_row = (target == 16 * half + 8 + b // 2) & (a == 15)
     for i, (low, high) in enumerate(((None, average), (low_col, high_col), (low_row, high_row))):
         values = jnp.where(high, 0.125, 0.0)
         if low is not None:
@@ -289,20 +290,27 @@
 
 def pack_results(u, edges, weights, held, packed):
     thick = [u[i // 2][2 * (i % 2)] + u[i // 2][2 * (i % 2) + 1] for i in range(IMAGES)]
-    inner = select_dot(thick, weights[0])
-    inner = inner + select_dot(edges[1], weights[1])
-    outer = select_dot(edges[0], weights[2])
-    inner = [inner[8 * i : 8 * i + 8] for i in range(IMAGES)]
-    outer = [outer[8 * i : 8 * i + 8] for i in range(IMAGES)]
+
+    def pairs(values, i):
+        rows = [jnp.concatenate(values[2 * p : 2 * p + 2], axis=1) for p in range(5)]
+        sums = select_dot(rows, weights[i])
+        return [sums[8 * p : 8 * p + 8] for p in range(5)]
+
+    inner, cols, rows = pairs(thick, 0), pairs(edges[1], 1), pairs(edges[0], 2)
     lane = iota((BOXES, LANES), 1)
+    first_cols = cols[0]
+    for p in range(1, 4):
+        first_cols = jnp.where(lane % 16 // 4 == p, roll(cols[p], 4 * p, 1), first_cols)
     for i in range(8):
-        message = roll(outer[i], 100, 1)
+        message = roll(cols[4], 120 - 16 * i, 1)
+        message = jnp.where(lane < 120, roll(first_cols, 104 - 16 * i, 1), message)
         if i < 4:
-            last = roll(outer[8 + i % 2], 116 if i < 2 else 108, 1)
-            message = jnp.where(lane < 116, message, last)
-        for image in range(IMAGES - 1, -1, -1):
-            part = roll(inner[image], 10 * image - 16 * i, 1)
-            message = jnp.where(lane < 10 * image + 10, part, message)
+            start = 16 * (i % 2) + 8 * (i // 2)
+            message = jnp.where(lane < 104, roll(rows[4], 96 - start, 1), message)
+        message = jnp.where(lane < 96, roll(rows[i // 2], 80 - 16 * (i % 2), 1), message)
+        for p in range(4, -1, -1):
+            part = roll(inner[p], 16 * (p - i), 1)
+            message = jnp.where(lane < 16 * p + 16, part, message)
         held[pl.ds(i, BOXES, stride=8), :] = message
     for r in range(BOXES):
         packed[r] = held[pl.ds(8 * r, 8), :]
@@ -506,11 +514,12 @@
     wanted,
     out,
     slots,
-    marks,
-    outer,
-    inner,
+    covered_in,
+    turned,
+    fine,
     sems,
     out_sem,
+    fine_sem,
 ):
     pairs = (
         (wanted_in, wanted),
@@ -518,7 +527,7 @@
         (new_in, new),
         (flux_x_in, flux_x),
         (flux_y_in, flux_y),
-        (fine_in, fine_out),
+        (fine_in, fine),
     )
     loads = [pltpu.make_async_copy(a, b, sems.at[i]) for i, (a, b) in enumerate(pairs)]
     for copy in loads:
@@ -537,40 +546,33 @@
     loads[0].wait()
     lax.fori_loop(0, n, place, 0, unroll=8)
     blank = jnp.zeros((8, LANES), jnp.float32)
+    group = lane // 8
     for tx in (0, 7):
-        for i in range(2):
-            marks[tx, i] = blank
-        for image in range(IMAGES):
-            inner[tx, image] = blank
-        for g in range(3):
-            outer[tx, g] = blank
+        covered_in[tx] = blank
+        for i in range(16):
+            turned[tx, i] = blank
+    loads[5].wait()
+    store_fine = pltpu.make_async_copy(fine, fine_out, fine_sem)
+    store_fine.start()
 
     def row_of_tiles(tx, carry):
-        parts = [blank] * IMAGES
-        sides = [blank] * 3
-        covered, touched = blank, blank
-        before = jnp.int32(0)
+        covered = blank
+        diagonals = [blank] * 16
         for ty in range(1, 15):
             slot = slots[16 * tx + ty]
             live = (slot >= 0).astype(jnp.int32)
             message = returned[jnp.maximum(slot, 0)]
-            here = (lane // 8 == ty) & (lane < 1024 * live)
-            first = jnp.where(live > 0, 8 * ty - 1 + before, 1024)
-            wide = (lane >= first) & (lane < 8 * ty + 9)
-            covered = jnp.where(here, 1.0, covered)
-            touched = jnp.where(wide, 1.0, touched)
-            for image in range(IMAGES):
-                turned = roll(message, 8 * ty - 1 - 10 * image, 1)
-                parts[image] = jnp.where(wide, turned, parts[image])
-            for g in range(3):
-                sides[g] = jnp.where(here, roll(message, 8 * ty - 100 - 8 * g, 1), sides[g])
-            before = live
-        marks[tx, 0] = covered
-        marks[tx, 1] = touched
-        for image in range(IMAGES):
-            inner[tx, image] = parts[image]
-        for g in range(3):
-            outer[tx, g] = sides[g]
+            covered = jnp.where(lane // 8 == jnp.where(live > 0, ty, -1), 1.0, covered)
+            for d in range(16):
+                i = (ty - d) % 16
+                diagonals[d] = jnp.where(group == i, message, diagonals[d])
+        diagonals = [roll(diagonals[d], 8 * d, 1) for d in range(16)]
+        covered_in[tx] = covered
+        for i in range(16):
+            part = blank
+            for ty in range(1, 15):
+                part = jnp.where(group == ty, diagonals[(ty - i) % 16], part)
+            turned[tx, i] = part
         return carry
 
     loads[1].wait()
@@ -580,27 +582,32 @@
 
     def finish(tx, carry):
         above, below = jnp.minimum(tx + 1, 7), jnp.maximum(tx - 1, 0)
-        covered = marks[tx, 0] > 0.5
-        touched = marks[tx, 1] > 0.5
-        beside = (sub == 7) & (marks[above, 0] > 0.5) | (sub == 0) & (marks[below, 0] > 0.5)
+        cover = covered_in[tx]
+        covered = cover > 0.5
+        last = lane % 8 == 7
+        touched = last & (roll(cover, -1, 1) > 0.5) | (lane % 8 == 0) & (roll(cover, 1, 1) > 0.5)
+        beside = (sub == 7) & (covered_in[above] > 0.5) | (sub == 0) & (covered_in[below] > 0.5)
         rows = pl.ds(pl.multiple_of(8 * tx, 8), 8)
-        low, high = [outer[above, g] for g in range(3)], [outer[below, g] for g in range(3)]
+        low, high = [turned[above, 10 + g] for g in range(3)], [turned[below, 10 + g] for g in range(3)]
+        cols = [turned[tx, 13 + g] for g in range(3)]
         for image in range(IMAGES):
             if image < 8:
                 lows, highs = low[0][image : image + 1], high[1][image : image + 1]
             else:
                 lows, highs = low[2][image - 8 : image - 7], high[2][image - 6 : image - 5]
-            value = inner[tx, image]
+            place = 2 * (image % 4)
+            value = cols[image // 4]
+            value = jnp.where(last, roll(value, -1 - place, 1), roll(value, 7 - place, 1))
             cells = new[image, rows, :] + jnp.where(touched, value - flux_y[image, rows, :], 0.0)
             faces = jnp.where(sub == 7, lows, highs)
             cells = cells + jnp.where(beside, faces - flux_x[image, rows, :], 0.0)
-            out[image, rows, :] = jnp.where(covered, value, cells)
+            out[image, rows, :] = jnp.where(covered, turned[tx, image], cells)
         pltpu.make_async_copy(out.at[:, rows], out_to.at[:, rows], out_sem).start()
         return carry
 
     lax.fori_loop(0, 8, finish, 0)
     pltpu.make_async_copy(out, out_to, out_sem).wait()
-    loads[5].wait()
+    store_fine.wait()
 
 
 def body(n, m, coarse_state, fine_state, source_rows, tile_ids):
@@ -649,7 +656,7 @@
             pltpu.VMEM((2, 32, LANES), f32),
             pltpu.VMEM((2, ROWS, LANES), f32),
             pltpu.VMEM((2, LANES, 256), jnp.bfloat16),
-            pltpu.VMEM((3, 256, LANES), jnp.bfloat16),
+            pltpu.VMEM((3, 512, LANES), jnp.bfloat16),
             pltpu.SemaphoreType.DMA((4,)),
             pltpu.SemaphoreType.DMA((6,)),
             pltpu.SemaphoreType.DMA((2,)),
@@ -676,10 +683,11 @@
             pltpu.SMEM((n,), jnp.int32),
             field,
             pltpu.SMEM((128,), jnp.int32),
-            pltpu.VMEM((8, 2, 8, LANES), f32),
-            pltpu.VMEM((8, 3, 8, LANES), f32),
-            pltpu.VMEM((8, IMAGES, 8, LANES), f32),
+            pltpu.VMEM((8, 8, LANES), f32),
+            pltpu.VMEM((8, 16, 8, LANES), f32),
+            pltpu.VMEM((BOXES, 5, 4, 256), f32),
             pltpu.SemaphoreType.DMA((6,)),
+            pltpu.SemaphoreType.DMA,
             pltpu.SemaphoreType.DMA,
         ],
         compiler_params=pltpu.CompilerParams(vmem_limit_bytes=VMEM_LIMIT),

time: 48.7 us -> 46.6 us (0.957)
  Pallas kernels: 47.9 us -> 45.8 us
    pallas_call x1, Pallas kernels: 6.14 us -> 3.87 us  [body(): pl.pallas_call(functools.partial(merge_kernel, n), out_shape=(stack, boxe...]
where the time goes in v3:
time: 46.6 us; the launch traced here: 46.5 us
  Pallas kernels  45.8 us (98%)
  between operations  0.64 us (1%)
    pallas_call x1, Pallas kernels, body(): pl.pallas_call(functools.partial(level_kernel, n, m), out_shape=(image, i...  41.9 us
    pallas_call x1, Pallas kernels, body(): pl.pallas_call(functools.partial(merge_kernel, n), out_shape=(stack, boxe...  3.87 us

profile of v3, /device:TPU:14, one launch (start us, length us, event | category | flops | bytes accessed | tf_op | source)
XLA Modules:
  0.0 46.5 jit_solution(12936961060268989511)
XLA Ops:
  0.6 41.9 %levels.1 = (f32[640,128]{1,0:T(8,128)}, f32[640,128]{1,0:T(8,128)}, f32[640,128]{1,0:T(8,128)}, f32[64,8,128]{2,1,0:T(8,128)}, f32[8,5,4,256]{3,2,1,0:T(4,128)}, /*index=5*/s32[64]{0:T(128)}) custom-call(f32[640,128]{1,0:T(8,128)} %bitcast.16, f32[8,5,4,256]{3,2,1,0:T(4,128)} %bitcast.17, s32[8,64]{1,0:T(8,128)} %bitcast.18, s32[8,64]{1,0:T(8,128)} %bitcast.19), custom_call_target="tpu_custom_call" | custom-call | tf_op jit(solution)/shard_map/levels/pallas_call | solution.py:623
  42.6 3.9 %merge.1 = (f32[10,64,128]{2,1,0:T(8,128)}, f32[8,5,4,256]{3,2,1,0:T(4,128)}) custom-call(f32[10,64,128]{2,1,0:T(8,128)} %bitcast.13, f32[10,64,128]{2,1,0:T(8,128)} %bitcast.14, f32[10,64,128]{2,1,0:T(8,128)} %bitcast.15, f32[64,8,128]{2,1,0:T(8,128)} %get-tuple-element.13.returned_in, s32[64]{0:T(128)} %get-tuple-element.14.wanted_in, ...), custom_call_target="tpu_custom_call" | custom-call | tf_op jit(solution)/shard_map/merge/pallas_call | solution.py:673

commit v4 on v3

--- a/solution.py
+++ b/solution.py
@@ -99,15 +99,16 @@
 def build_tables(img, turned, table_x, table_y):
     for tx in range(1, 7):
         for k, row in ((0, 8 * tx - 1), (1, 8 * tx + 8)):
-            table_x[tx, pl.ds(16 * k, 8), :] = img[pl.ds(row, 8, stride=ROWS), :]
-            table_x[tx, pl.ds(16 * k + 8, 8), :] = img[pl.ds(8 * ROWS + row, 8, stride=ROWS), :]
-            table_x[tx, pl.ds(32 + 4 * k, 4), :] = img[pl.ds(16 * ROWS + row, 4, stride=ROWS), :]
+            for q in range(4):
+                rows = img[pl.ds(5 * q * ROWS + row, 5, stride=ROWS), :]
+                table_x[tx, 4 * k + q, pl.ds(0, 5), :] = rows
     for p in range(IMAGES):
         turned[pl.ds(p * LANES, LANES), :] = jnp.transpose(img[pl.ds(p * LANES, LANES), :])
     for ty in range(1, 15):
         for k, col in ((0, 8 * ty - 1), (1, 8 * ty + 8)):
-            table_y[ty, pl.ds(8 * k, 8), :] = turned[pl.ds(col, 8, stride=LANES), :]
-            table_y[ty, pl.ds(16 + 2 * k, 2), :] = turned[pl.ds(8 * LANES + col, 2, stride=LANES), :]
+            for h in range(2):
+                rows = turned[pl.ds(5 * h * LANES + col, 5, stride=LANES), :]
+                table_y[ty, 2 * k + h, pl.ds(0, 5), :] = rows
 
 
 def wanted_tile(sources, tiles, o, me):
@@ -121,16 +122,16 @@
     group = iota((8, LANES), 1) // 8
     for tx in range(1, 7):
         for ty in range(1, 15):
-            message = jnp.zeros((8, LANES), jnp.float32)
-            for g in range(5):
-                part = roll(table_x[tx, pl.ds(8 * g, 8), :], 8 * g - 8 * ty, 1)
+            message = roll(table_x[tx, 0], -8 * ty, 1)
+            for g in range(1, 8):
+                part = roll(table_x[tx, g], 8 * g - 8 * ty, 1)
                 message = jnp.where(group == g, part, message)
-            for u in range(3):
-                columns = table_y[ty, pl.ds(8 * u, 8), :]
+            for u in range(4):
+                columns = table_y[ty, u]
                 for j in range(2):
                     part = roll(columns, 64 + 16 * u + 8 * j - 64 * j - 8 * tx, 1)
                     message = jnp.where(group == 8 + 2 * u + j, part, message)
-            by_tile[16 * tx + ty] = message
+            by_tile[16 * tx + ty] = message[:5]
 
     def one(o, carry):
         tile = wanted_tile(sources, tiles, o, me)
@@ -221,8 +222,8 @@
 
 def own_rims(me, sources, rims, held, weights):
     for r in range(BOXES):
-        held[pl.ds(8 * r, 8), :] = rims[sources[r, me]]
-    by_row = [held[pl.ds(s, BOXES, stride=8), :] for s in range(8)]
+        held[pl.ds(8 * r, 5), :] = rims[sources[r, me]]
+    by_row = [held[pl.ds(s, BOXES, stride=8), :] for s in range(5)]
     lane = iota((BOXES, LANES), 1)
 
     def pair(low, low_lane, high, high_lane):
@@ -232,16 +233,11 @@
 
     sides = [[], []]
     for image in range(2 * IMAGES):
-        s, g = image % 8, image // 8
-        if g < 2:
-            sides[0].append(pair(by_row[s], 8 * g, by_row[s], 8 * (g + 2)))
-        else:
-            sides[0].append(pair(by_row[s], 32, by_row[s + 4], 32))
+        row, q = by_row[image % 5], image // 5
+        sides[0].append(pair(row, 8 * q, row, 32 + 8 * q))
         p, j = image // 2, image % 2
-        if p < 8:
-            sides[1].append(pair(by_row[p], 64 + 8 * j, by_row[p], 80 + 8 * j))
-        else:
-            sides[1].append(pair(by_row[p - 8], 96 + 8 * j, by_row[p - 6], 96 + 8 * j))
+        row, lane_j = by_row[p % 5], 16 * (p // 5) + 8 * j
+        sides[1].append(pair(row, 64 + lane_j, row, 96 + lane_j))
 
     spread = []
     for side in range(2):
@@ -359,7 +355,7 @@
     sources_in,
     tiles_in,
     coarse_new,
-    flux_x_out,
+    rows_x_out,
     flux_y_out,
     returned,
     fine_out,
@@ -371,6 +367,7 @@
     img,
     flux_x,
     flux_y,
+    rows_x,
     fine,
     turned,
     table_x,
@@ -415,8 +412,12 @@
     load_fine.start()
     load.wait()
     coarse_step(img, flux_x, flux_y)
+    for image in range(IMAGES):
+        for i in range(2):
+            rows = flux_x[pl.ds(image * ROWS + 7 * i, 8, stride=8), :]
+            rows_x[image, pl.ds(8 * i, 8), :] = rows
     stores = [
-        pltpu.make_async_copy(flux_x, flux_x_out, store_sems.at[0]),
+        pltpu.make_async_copy(rows_x, rows_x_out, store_sems.at[0]),
         pltpu.make_async_copy(flux_y, flux_y_out, store_sems.at[1]),
     ]
     stores[0].start()
@@ -500,7 +501,7 @@
 def merge_kernel(
     n,
     new_in,
-    flux_x_in,
+    rows_x_in,
     flux_y_in,
     returned_in,
     wanted_in,
@@ -508,7 +509,7 @@
     out_to,
     fine_out,
     new,
-    flux_x,
+    rows_x,
     flux_y,
     returned,
     wanted,
@@ -525,7 +526,7 @@
         (wanted_in, wanted),
         (returned_in, returned),
         (new_in, new),
-        (flux_x_in, flux_x),
+        (rows_x_in, rows_x),
         (flux_y_in, flux_y),
         (fine_in, fine),
     )
@@ -599,8 +600,9 @@
             value = cols[image // 4]
             value = jnp.where(last, roll(value, -1 - place, 1), roll(value, 7 - place, 1))
             cells = new[image, rows, :] + jnp.where(touched, value - flux_y[image, rows, :], 0.0)
-            faces = jnp.where(sub == 7, lows, highs)
-            cells = cells + jnp.where(beside, faces - flux_x[image, rows, :], 0.0)
+            lows = lows - rows_x[image, pl.ds(8 + tx, 1), :]
+            highs = highs - rows_x[image, pl.ds(tx, 1), :]
+            cells = cells + jnp.where(beside, jnp.where(sub == 7, lows, highs), 0.0)
             out[image, rows, :] = jnp.where(covered, turned[tx, image], cells)
         pltpu.make_async_copy(out.at[:, rows], out_to.at[:, rows], out_sem).start()
         return carry
@@ -620,11 +622,11 @@
     shape = jax.ShapeDtypeStruct
     image = shape((IMAGES * ROWS, LANES), f32)
     boxes = shape((BOXES, 5, 4, 256), f32)
-    new, flux_x, flux_y, returned, fine_out, wanted = pl.pallas_call(
+    new, rows_x, flux_y, returned, fine_out, wanted = pl.pallas_call(
         functools.partial(level_kernel, n, m),
         out_shape=(
             image,
-            image,
+            shape((IMAGES, 16, LANES), f32),
             image,
             shape((n, 8, LANES), f32),
             boxes,
@@ -640,13 +642,14 @@
             pltpu.VMEM((2 * IMAGES * ROWS, LANES), f32),
             pltpu.VMEM((IMAGES * ROWS, LANES), f32),
             pltpu.VMEM((IMAGES * ROWS, LANES), f32),
+            pltpu.VMEM((IMAGES, 16, LANES), f32),
             pltpu.VMEM((BOXES, 5, 4, 256), f32),
             pltpu.VMEM((IMAGES * LANES, LANES), f32),
-            pltpu.VMEM((8, 40, LANES), f32),
-            pltpu.VMEM((16, 24, LANES), f32),
-            pltpu.VMEM((128, 8, LANES), f32),
-            pltpu.VMEM((n, 8, LANES), f32),
-            pltpu.VMEM((n, 8, LANES), f32),
+            pltpu.VMEM((8, 8, 8, LANES), f32),
+            pltpu.VMEM((16, 4, 8, LANES), f32),
+            pltpu.VMEM((128, 5, LANES), f32),
+            pltpu.VMEM((n, 5, LANES), f32),
+            pltpu.VMEM((n, 5, LANES), f32),
             pltpu.VMEM((8 * BOXES, LANES), f32),
             pltpu.VMEM((BOXES, 8, LANES), f32),
             pltpu.VMEM((n, 8, LANES), f32),
@@ -677,7 +680,7 @@
         out_specs=(hbm,) * 2,
         scratch_shapes=[
             field,
-            field,
+            pltpu.VMEM((IMAGES, 16, LANES), f32),
             field,
             pltpu.VMEM((n, 8, LANES), f32),
             pltpu.SMEM((n,), jnp.int32),
@@ -694,7 +697,7 @@
         name="merge",
     )(
         new.reshape(stack.shape),
-        flux_x.reshape(stack.shape),
+        rows_x,
         flux_y.reshape(stack.shape),
         returned,
         wanted,

time: 46.6 us -> 45.1 us (0.968)
  Pallas kernels: 45.8 us -> 44.3 us
    pallas_call x1, Pallas kernels: 41.9 us -> 40.5 us  [body(): pl.pallas_call(functools.partial(level_kernel, n, m), out_shape=(image, s...]
where the time goes in v4:
time: 45.1 us; the launch traced here: 44.9 us
  Pallas kernels  44.3 us (98%)
  between operations  0.64 us (1%)
    pallas_call x1, Pallas kernels, body(): pl.pallas_call(functools.partial(level_kernel, n, m), out_shape=(image, s...  40.5 us
    pallas_call x1, Pallas kernels, body(): pl.pallas_call(functools.partial(merge_kernel, n), out_shape=(stack, boxe...  3.8 us

profile of v4, /device:TPU:14, one launch (start us, length us, event | category | flops | bytes accessed | tf_op | source)
XLA Modules:
  0.0 44.9 jit_solution(15473596274957875853)
XLA Ops:
  0.6 40.5 %levels.1 = (f32[640,128]{1,0:T(8,128)}, f32[10,16,128]{2,1,0:T(8,128)}, f32[640,128]{1,0:T(8,128)}, f32[64,8,128]{2,1,0:T(8,128)}, f32[8,5,4,256]{3,2,1,0:T(4,128)}, /*index=5*/s32[64]{0:T(128)}) custom-call(f32[640,128]{1,0:T(8,128)} %bitcast.12, f32[8,5,4,256]{3,2,1,0:T(4,128)} %bitcast.15, s32[8,64]{1,0:T(8,128)} %bitcast.16, s32[8,64]{1,0:T(8,128)} %bitcast.17), custom_call_target="tpu_custom_call" | custom-call | tf_op jit(solution)/shard_map/levels/pallas_call | solution.py:625
  41.1 3.8 %merge.1 = (f32[10,64,128]{2,1,0:T(8,128)}, f32[8,5,4,256]{3,2,1,0:T(4,128)}) custom-call(f32[10,64,128]{2,1,0:T(8,128)} %bitcast.13, f32[10,16,128]{2,1,0:T(8,128)} %get-tuple-element.11.rows_x_in, f32[10,64,128]{2,1,0:T(8,128)} %bitcast.14, f32[64,8,128]{2,1,0:T(8,128)} %get-tuple-element.13.returned_in, s32[64]{0:T(128)} %get-tuple-element.14.wanted_in, ...), custom_call_target="tpu_custom_call" | custom-call | tf_op jit(solution)/shard_map/merge/pallas_call | solution.py:676

commit v5 on v4

--- a/solution.py
+++ b/solution.py
@@ -552,32 +552,32 @@
         covered_in[tx] = blank
         for i in range(16):
             turned[tx, i] = blank
+
+    def row_of_tiles(tx, carry):
+        covered = blank
+        parts = [blank] * 16
+        for ty in range(1, 15):
+            slot = slots[16 * tx + ty]
+            live = (slot >= 0).astype(jnp.int32)
+            parts[ty] = returned[jnp.maximum(slot, 0)]
+            covered = jnp.where(group == jnp.where(live > 0, ty, -1), 1.0, covered)
+        for step in (8, 4, 2, 1):
+            kept = group // step % 2 == 0
+            for i in range(16):
+                if i // step % 2 == 0:
+                    low, high = parts[i], parts[i + step]
+                    parts[i] = jnp.where(kept, low, roll(high, 8 * step, 1))
+                    parts[i + step] = jnp.where(kept, roll(low, -8 * step, 1), high)
+        covered_in[tx] = covered
+        for i in range(16):
+            turned[tx, i] = parts[i]
+        return carry
+
+    loads[1].wait()
+    lax.fori_loop(1, 7, row_of_tiles, 0)
     loads[5].wait()
     store_fine = pltpu.make_async_copy(fine, fine_out, fine_sem)
     store_fine.start()
-
-    def row_of_tiles(tx, carry):
-        covered = blank
-        diagonals = [blank] * 16
-        for ty in range(1, 15):
-            slot = slots[16 * tx + ty]
-            live = (slot >= 0).astype(jnp.int32)
-            message = returned[jnp.maximum(slot, 0)]
-            covered = jnp.where(lane // 8 == jnp.where(live > 0, ty, -1), 1.0, covered)
-            for d in range(16):
-                i = (ty - d) % 16
-                diagonals[d] = jnp.where(group == i, message, diagonals[d])
-        diagonals = [roll(diagonals[d], 8 * d, 1) for d in range(16)]
-        covered_in[tx] = covered
-        for i in range(16):
-            part = blank
-            for ty in range(1, 15):
-                part = jnp.where(group == ty, diagonals[(ty - i) % 16], part)
-            turned[tx, i] = part
-        return carry
-
-    loads[1].wait()
-    lax.fori_loop(1, 7, row_of_tiles, 0)
     for copy in loads[2:5]:
         copy.wait()
 

time: 45.1 us -> 45.6 us (1.011)
  Pallas kernels: 44.3 us -> 44.8 us
    pallas_call x1, Pallas kernels: 3.8 us -> 4.33 us  [body(): pl.pallas_call(functools.partial(merge_kernel, n), out_shape=(stack, boxe...]
where the time goes in v5:
time: 45.6 us; the launch traced here: 45.4 us
  Pallas kernels  44.8 us (98%)
  between operations  0.64 us (1%)
    pallas_call x1, Pallas kernels, body(): pl.pallas_call(functools.partial(level_kernel, n, m), out_shape=(image, s...  40.5 us
    pallas_call x1, Pallas kernels, body(): pl.pallas_call(functools.partial(merge_kernel, n), out_shape=(stack, boxe...  4.33 us

profile of v5, /device:TPU:14, one launch (start us, length us, event | category | flops | bytes accessed | tf_op | source)
XLA Modules:
  0.0 45.4 jit_solution(6424727506893400161)
XLA Ops:
  0.6 40.5 %levels.1 = (f32[640,128]{1,0:T(8,128)}, f32[10,16,128]{2,1,0:T(8,128)}, f32[640,128]{1,0:T(8,128)}, f32[64,8,128]{2,1,0:T(8,128)}, f32[8,5,4,256]{3,2,1,0:T(4,128)}, /*index=5*/s32[64]{0:T(128)}) custom-call(f32[640,128]{1,0:T(8,128)} %bitcast.12, f32[8,5,4,256]{3,2,1,0:T(4,128)} %bitcast.15, s32[8,64]{1,0:T(8,128)} %bitcast.16, s32[8,64]{1,0:T(8,128)} %bitcast.17), custom_call_target="tpu_custom_call" | custom-call | tf_op jit(solution)/shard_map/levels/pallas_call | solution.py:625
  41.1 4.3 %merge.1 = (f32[10,64,128]{2,1,0:T(8,128)}, f32[8,5,4,256]{3,2,1,0:T(4,128)}) custom-call(f32[10,64,128]{2,1,0:T(8,128)} %bitcast.13, f32[10,16,128]{2,1,0:T(8,128)} %get-tuple-element.11.rows_x_in, f32[10,64,128]{2,1,0:T(8,128)} %bitcast.14, f32[64,8,128]{2,1,0:T(8,128)} %get-tuple-element.13.returned_in, s32[64]{0:T(128)} %get-tuple-element.14.wanted_in, ...), custom_call_target="tpu_custom_call" | custom-call | tf_op jit(solution)/shard_map/merge/pallas_call | solution.py:676

commit v6 on v4

--- a/solution.py
+++ b/solution.py
@@ -552,9 +552,6 @@
         covered_in[tx] = blank
         for i in range(16):
             turned[tx, i] = blank
-    loads[5].wait()
-    store_fine = pltpu.make_async_copy(fine, fine_out, fine_sem)
-    store_fine.start()
 
     def row_of_tiles(tx, carry):
         covered = blank
@@ -570,14 +567,17 @@
         diagonals = [roll(diagonals[d], 8 * d, 1) for d in range(16)]
         covered_in[tx] = covered
         for i in range(16):
-            part = blank
-            for ty in range(1, 15):
+            part = diagonals[(1 - i) % 16]
+            for ty in range(2, 15):
                 part = jnp.where(group == ty, diagonals[(ty - i) % 16], part)
             turned[tx, i] = part
         return carry
 
     loads[1].wait()
-    lax.fori_loop(1, 7, row_of_tiles, 0)
+    lax.fori_loop(1, 7, row_of_tiles, 0, unroll=6)
+    loads[5].wait()
+    store_fine = pltpu.make_async_copy(fine, fine_out, fine_sem)
+    store_fine.start()
     for copy in loads[2:5]:
         copy.wait()
 
@@ -607,7 +607,7 @@
         pltpu.make_async_copy(out.at[:, rows], out_to.at[:, rows], out_sem).start()
         return carry
 
-    lax.fori_loop(0, 8, finish, 0)
+    lax.fori_loop(0, 8, finish, 0, unroll=8)
     pltpu.make_async_copy(out, out_to, out_sem).wait()
     store_fine.wait()
 

time: 45.1 us -> 43.7 us (0.969)
  Pallas kernels: 44.3 us -> 42.9 us
    pallas_call x1, Pallas kernels: 3.8 us -> 2.39 us  [body(): pl.pallas_call(functools.partial(merge_kernel, n), out_shape=(stack, boxe...]
where the time goes in v6:
time: 43.7 us; the launch traced here: 43.5 us
  Pallas kernels  42.9 us (98%)
  between operations  0.64 us (1%)
    pallas_call x1, Pallas kernels, body(): pl.pallas_call(functools.partial(level_kernel, n, m), out_shape=(image, s...  40.5 us
    pallas_call x1, Pallas kernels, body(): pl.pallas_call(functools.partial(merge_kernel, n), out_shape=(stack, boxe...  2.39 us

profile of v6, /device:TPU:14, one launch (start us, length us, event | category | flops | bytes accessed | tf_op | source)
XLA Modules:
  0.0 43.5 jit_solution(10706938401469339535)
XLA Ops:
  0.6 40.5 %levels.1 = (f32[640,128]{1,0:T(8,128)}, f32[10,16,128]{2,1,0:T(8,128)}, f32[640,128]{1,0:T(8,128)}, f32[64,8,128]{2,1,0:T(8,128)}, f32[8,5,4,256]{3,2,1,0:T(4,128)}, /*index=5*/s32[64]{0:T(128)}) custom-call(f32[640,128]{1,0:T(8,128)} %bitcast.12, f32[8,5,4,256]{3,2,1,0:T(4,128)} %bitcast.15, s32[8,64]{1,0:T(8,128)} %bitcast.16, s32[8,64]{1,0:T(8,128)} %bitcast.17), custom_call_target="tpu_custom_call" | custom-call | tf_op jit(solution)/shard_map/levels/pallas_call | solution.py:625
  41.1 2.4 %merge.1 = (f32[10,64,128]{2,1,0:T(8,128)}, f32[8,5,4,256]{3,2,1,0:T(4,128)}) custom-call(f32[10,64,128]{2,1,0:T(8,128)} %bitcast.13, f32[10,16,128]{2,1,0:T(8,128)} %get-tuple-element.11.rows_x_in, f32[10,64,128]{2,1,0:T(8,128)} %bitcast.14, f32[64,8,128]{2,1,0:T(8,128)} %get-tuple-element.13.returned_in, s32[64]{0:T(128)} %get-tuple-element.14.wanted_in, ...), custom_call_target="tpu_custom_call" | custom-call | tf_op jit(solution)/shard_map/merge/pallas_call | solution.py:676

commit v7 on v6

--- a/solution.py
+++ b/solution.py
@@ -143,7 +143,7 @@
         box_of[o] = box
         return carry
 
-    lax.fori_loop(0, n, one, 0)
+    lax.fori_loop(0, n, one, 0, unroll=8)
 
 
 def pack_halo(img, halo_rows, halo_cols):
@@ -431,18 +431,11 @@
     rims_in[me] = rims[me]
     stores.append(pltpu.make_async_copy(wanted, wanted_out, store_sems.at[2]))
     stores[2].start()
-    pack_halo(img, halo_rows, halo_cols)
-    load_fine.wait()
-    for r in range(BOXES):
-        for f in range(5):
-            for z in range(4):
-                cells[4 * f + z, pl.ds(r, 1), :] = fine[r, f, pl.ds(z, 1), :]
-    spread_weights(spread)
-    gather_weights(gather)
     pl.semaphore_wait(barrier, n + 1)
 
     for other in partners(n, me):
         send(me, other, rims, rims_in, rim_sems)
+    pack_halo(img, halo_rows, halo_cols)
     halos = []
     for i, (source, target, where) in enumerate(
         (
@@ -462,6 +455,13 @@
         )
         copy.start()
         halos.append(copy)
+    load_fine.wait()
+    for r in range(BOXES):
+        for f in range(5):
+            for z in range(4):
+                cells[4 * f + z, pl.ds(r, 1), :] = fine[r, f, pl.ds(z, 1), :]
+    spread_weights(spread)
+    gather_weights(gather)
 
     rim_copies = all_slots(n, me, rims, rims_in, rim_sems)
     rim_copies.wait_recv()

time: 43.7 us -> 42.7 us (0.977)
  Pallas kernels: 42.9 us -> 41.9 us
    pallas_call x1, Pallas kernels: 40.5 us -> 39.5 us  [body(): pl.pallas_call(functools.partial(level_kernel, n, m), out_shape=(image, s...]
where the time goes in v7:
time: 42.7 us; the launch traced here: 42.5 us
  Pallas kernels  41.9 us (98%)
  between operations  0.64 us (1%)
    pallas_call x1, Pallas kernels, body(): pl.pallas_call(functools.partial(level_kernel, n, m), out_shape=(image, s...  39.5 us
    pallas_call x1, Pallas kernels, body(): pl.pallas_call(functools.partial(merge_kernel, n), out_shape=(stack, boxe...  2.39 us

profile of v7, /device:TPU:14, one launch (start us, length us, event | category | flops | bytes accessed | tf_op | source)
XLA Modules:
  0.0 42.5 jit_solution(4450628008404116394)
XLA Ops:
  0.6 39.5 %levels.1 = (f32[640,128]{1,0:T(8,128)}, f32[10,16,128]{2,1,0:T(8,128)}, f32[640,128]{1,0:T(8,128)}, f32[64,8,128]{2,1,0:T(8,128)}, f32[8,5,4,256]{3,2,1,0:T(4,128)}, /*index=5*/s32[64]{0:T(128)}) custom-call(f32[640,128]{1,0:T(8,128)} %bitcast.12, f32[8,5,4,256]{3,2,1,0:T(4,128)} %bitcast.15, s32[8,64]{1,0:T(8,128)} %bitcast.16, s32[8,64]{1,0:T(8,128)} %bitcast.17), custom_call_target="tpu_custom_call" | custom-call | tf_op jit(solution)/shard_map/levels/pallas_call | solution.py:625
  40.1 2.4 %merge.1 = (f32[10,64,128]{2,1,0:T(8,128)}, f32[8,5,4,256]{3,2,1,0:T(4,128)}) custom-call(f32[10,64,128]{2,1,0:T(8,128)} %bitcast.13, f32[10,16,128]{2,1,0:T(8,128)} %get-tuple-element.11.rows_x_in, f32[10,64,128]{2,1,0:T(8,128)} %bitcast.14, f32[64,8,128]{2,1,0:T(8,128)} %get-tuple-element.13.returned_in, s32[64]{0:T(128)} %get-tuple-element.14.wanted_in, ...), custom_call_target="tpu_custom_call" | custom-call | tf_op jit(solution)/shard_map/merge/pallas_call | solution.py:676
